TPU v7x, 128 devices: a whole 4x4x4 slice. The times are simulated.
128 devices in a mesh: dp: 32 (over y, x_hi, z), section: 4 (over x_lo, core).
Axes of the slice: x: 4 (x_hi: 2, x_lo: 2; x = x_hi * 2 + x_lo), y: 4, z: 4, core: 2. Of those that a mesh axis runs over, the one named last changes fastest.
Arguments:
- section_inputs: bfloat16 [4, 12288, 3072], P('section', 'dp'), may hold values from -6 to 6
- weights: bfloat16 [4, 3072, 3072], P('section'), may hold values from -0.109375 to 0.109375
- output_grads: bfloat16 [4, 12288, 3072], P('section', 'dp'), may hold values from -3 to 3
- warm_start: bfloat16 [4, 8, 3072], P('section'), may hold values from -0.109375 to 0.109375
Outputs:
- arrived: bfloat16 [4, 12288, 3072], P('section', 'dp')
- left_factor: float32 [4, 8, 3072], P('section')
- right_factor: float32 [4, 8, 3072], P('section')
All inputs are finite; a program needn't handle non-finite values.
Results may differ from a plain program's by a relative error of at most 0.0085.
Values may be sent and summed in bfloat16 or wider, within the bound.
No kernel may reach another device: no remote copies, remote signals or barrier semaphores. Data moves between devices by JAX's collectives and lax.ppermute only.
A program may use at most 128 MiB of HBM per device.

v0:
```python
import jax
import jax.numpy as jnp
from jax import lax
from jax.sharding import PartitionSpec as P

MICRO = 4


def shifted(value, axis, steps):
    count = lax.axis_size(axis)
    initial, last = (max(0, -steps), min(count, count - steps))
    return lax.ppermute(value, axis, [(source, source + steps) for source in range(initial, last)])


def contract(left, right):
    return lax.dot_general(
        left, right, (((1,), (1,)), ((), ())), preferred_element_type=jnp.float32
    )


def split_product(factor, data, dims):
    upper = factor.astype(jnp.bfloat16)
    lower = (factor - upper.astype(jnp.float32)).astype(jnp.bfloat16)
    first = lax.dot_general(upper, data, (dims, ((), ())), preferred_element_type=jnp.float32)
    second = lax.dot_general(lower, data, (dims, ((), ())), preferred_element_type=jnp.float32)
    return first + second


def orthonormal(matrix):
    result = []
    for position in range(matrix.shape[0]):
        column = matrix[position]
        for earlier in result:
            column = column - jnp.sum(earlier * column) * earlier
        column = column * lax.rsqrt(jnp.sum(column * column) + 1e-06)
        result.append(column)
    return jnp.stack(result)


def per_device(section_inputs, weights, output_grads, warm_start):
    inputs_local = section_inputs[0]
    weight = weights[0]
    grads_local = output_grads[0]
    starting = warm_start[0]
    replicas = lax.axis_size("dp")
    projected = contract(starting, grads_local)
    partial_value = split_product(projected, inputs_local, ((1,), (0,)))
    left_factor = lax.psum(partial_value, "dp") / replicas
    basis = orthonormal(left_factor)
    block_rows = grads_local.shape[0] // MICRO
    pieces = []
    for block in range(MICRO):
        block_grad = grads_local[block * block_rows : (block + 1) * block_rows]
        gradient_block = contract(block_grad, weight).astype(jnp.bfloat16)
        pieces.append(shifted(gradient_block, "section", -1))
    arrived = jnp.concatenate(pieces, axis=0)
    backward = split_product(basis, inputs_local, ((1,), (1,)))
    right_partial = split_product(backward, grads_local, ((1,), (0,)))
    right_factor = lax.psum(right_partial, "dp") / replicas
    return (arrived[None], left_factor[None], right_factor[None])


def solution(mesh):
    return jax.shard_map(
        per_device,
        mesh=mesh,
        in_specs=(
            P("section", "dp", None),
            P("section", None, None),
            P("section", "dp", None),
            P("section", None, None),
        ),
        out_specs=(P("section", "dp", None), P("section", None, None), P("section", None, None)),
        check_vma=False,
    )
```

profile of v0, /device:TPU:0, one launch (start us, length us, event | category | flops | bytes accessed | tf_op | source)
XLA Modules:
  0.0 751.8 jit_solution(9597968230093292745)
XLA Ops:
  7.2 0.0 copy-start
  7.2 0.0 all-reduce.3.cloned.1.call-start
  7.2 13.4 %fusion.17 = bf16[96,3072]{1,0:T(8,128)(2,1)} fusion(bf16[1,3072,3072]{2,1,0:T(8,128)(2,1)} %param.5, bf16[1,384,3072]{2,1,0:T(8,128)(2,1)} %param.6), kind=kOutput, calls=%fused_computation.11 | convolution fusion | flops 1812234240 | bytes 20054016 | tf_op jit(solution)/shard_map/dot_general | solution.py:16
  20.6 0.0 copy-start.2
  20.6 1.4 collective-permute-start.3
  22.1 13.3 %fusion.14 = bf16[96,3072]{1,0:T(8,128)(2,1)} fusion(bf16[1,3072,3072]{2,1,0:T(8,128)(2,1)} %param.5, bf16[1,384,3072]{2,1,0:T(8,128)(2,1)} %param.6), kind=kOutput, calls=%fused_computation.10 | convolution fusion | flops 1812234240 | bytes 20054016 | tf_op jit(solution)/shard_map/dot_general | solution.py:16
  35.4 1.3 collective-permute-start.2
  36.6 0.0 copy-done.2
  36.7 2.4 fusion.30
  39.0 0.0 copy-done
  39.0 0.4 fusion.25
  39.5 1.1 convolution_add_fusion.1
  40.5 0.0 all-reduce.3.cloned.1.call-update
  40.6 0.2 all-reduce.5.cloned.1.call-start
  40.8 13.3 %fusion.11 = bf16[96,3072]{1,0:T(8,128)(2,1)} fusion(bf16[1,3072,3072]{2,1,0:T(8,128)(2,1)} %param.5, bf16[1,384,3072]{2,1,0:T(8,128)(2,1)} %param.6), kind=kOutput, calls=%fused_computation.9 | convolution fusion | flops 1812234240 | bytes 20054016 | tf_op jit(solution)/shard_map/dot_general | solution.py:16
  54.1 1.3 collective-permute-start.1
  55.4 305.9 %all-reduce.3.cloned.1.call-done = f32[8,3072]{1,0:T(8,128)} async-done(((f32[8,3072]{1,0:T(8,128)}), f32[8,3072]{1,0:T(8,128)}) %all-reduce.3.cloned.1.call-update) | async-done | bytes 98320 | tf_op jit(solution)/shard_map/psum | solution.py:48
  361.3 1.5 broadcast_multiply_fusion
  362.9 0.7 fusion.51
  364.2 0.6 multiply_reduce_fusion.34
  364.8 1.3 multiply_reduce_fusion.7
  366.8 5.0 multiply_reduce_fusion.6
  371.8 1.8 multiply_reduce_fusion.30
  374.3 1.9 multiply_reduce_fusion.27
  376.3 6.3 multiply_reduce_fusion.5
  383.2 3.8 multiply_reduce_fusion.4
  387.0 2.6 multiply_reduce_fusion.21
  390.3 5.1 multiply_reduce_fusion.3
  395.4 1.4 multiply_reduce_fusion.15
  397.5 2.0 multiply_reduce_fusion.2
  399.5 1.9 multiply_reduce_fusion.8
  402.1 2.0 multiply_reduce_fusion.1
  404.2 1.3 multiply_reduce_fusion
  406.1 18.0 %subtract_multiply_fusion = (f32[1,3072]{1,0:T(1,128)S(1)}, f32[1,3072]{1,0:T(1,128)S(1)}, f32[1,3072]{1,0:T(1,128)S(1)}, f32[1,3072]{1,0:T(1,128)S(1)}, f32[1,3...) fusion(f32[]{:T(128)S(6)} %rsqrt.31, f32[]{:T(128)} %get-tuple-element.37, f32[]{:T(128)} %get-tuple-element.3, ...), kind=kLoop, calls=%fused_computation.44 | loop fusion | flops 196608 | bytes 184464 | tf_op jit(solution)/shard_map/mul | solution.py:35
  424.1 0.2 stack.2
  424.2 0.0 copy-start.1
  424.2 0.7 fusion.20
  424.9 0.7 fusion.32
  425.7 0.2 copy-done.1
  425.9 0.4 fusion.28
  426.3 1.1 convolution_add_fusion
  427.4 0.0 all-reduce.5.cloned.1.call-update
  427.4 13.3 %fusion.8 = bf16[96,3072]{1,0:T(8,128)(2,1)} fusion(bf16[1,3072,3072]{2,1,0:T(8,128)(2,1)} %param.5, bf16[1,384,3072]{2,1,0:T(8,128)(2,1)} %param.6), kind=kOutput, calls=%fused_computation.8 | convolution fusion | flops 1812234240 | bytes 20054016 | tf_op jit(solution)/shard_map/dot_general | solution.py:16
  440.7 1.3 collective-permute-start
  442.0 298.3 %all-reduce.5.cloned.1.call-done = f32[8,3072]{1,0:T(8,128)} async-done(((f32[8,3072]{1,0:T(8,128)}), f32[8,3072]{1,0:T(8,128)}) %all-reduce.5.cloned.1.call-update) | async-done | bytes 98320 | tf_op jit(solution)/shard_map/psum | solution.py:59
  740.3 1.5 multiply_bitcast_fusion
  741.9 0.0 collective-permute-done.3
  741.9 0.0 collective-permute-done.2
  741.9 0.0 collective-permute-done.1
  741.9 0.0 collective-permute-done
  741.9 3.1 maximum_bitcast_fusion
  (1 shorter events, 0.0 us)
Async XLA Ops:
  7.2 31.9 %copy-start = (bf16[1,384,3072]{2,1,0:T(8,128)(2,1)S(1)}, bf16[1,384,3072]{2,1,0:T(8,128)(2,1)}, u32[]{:S(2)}) copy-start(bf16[1,384,3072]{2,1,0:T(8,128)(2,1)} %param.4) | copy-start | bytes 7077892
  7.2 354.1 %all-reduce.3.cloned.1.call-start = ((), (), s32[]{:S(2)}) async-start(), calls=%async_computation | async-start | bytes 196608 | tf_op jit(solution)/shard_map/psum | solution.py:48
  20.6 16.0 %copy-start.2 = (bf16[1,8,3072]{2,1,0:T(8,128)(2,1)S(1)}, bf16[1,8,3072]{2,1,0:T(8,128)(2,1)}, u32[]{:S(2)}) copy-start(bf16[1,8,3072]{2,1,0:T(8,128)(2,1)} %param.7) | copy-start | bytes 147460
  20.6 721.2 %collective-permute-start.3 = (bf16[96,3072]{1,0:T(8,128)(2,1)}, bf16[96,3072]{1,0:T(8,128)(2,1)S(1)}, u32[]{:S(2)}, u32[]{:S(2)}) collective-permute-start(bf16[96,3072]{1,0:T(8,128)(2,1)} %fusion.17), channel_id=1, source_target_pairs={{1,0},{2,1},{3,2},{5,4},{6,5},{7,6},{9,8},{10,9},{11,10},{13,12},{... | collective-permute-start | bytes 1769480 | tf_op jit(solution)/shard_map/ppermute | solution.py:12
  35.4 706.5 %collective-permute-start.2 = (bf16[96,3072]{1,0:T(8,128)(2,1)}, bf16[96,3072]{1,0:T(8,128)(2,1)}, u32[]{:S(2)}, u32[]{:S(2)}) collective-permute-start(bf16[96,3072]{1,0:T(8,128)(2,1)} %fusion.14), channel_id=1, source_target_pairs={{1,0},{2,1},{3,2},{5,4},{6,5},{7,6},{9,8},{10,9},{11,10},{13,12},{... | collective-permute-start | bytes 1769480 | tf_op jit(solution)/shard_map/ppermute | solution.py:12
  40.6 699.8 %all-reduce.5.cloned.1.call-start = ((), (), s32[]{:S(2)}) async-start(), calls=%async_computation.1 | async-start | bytes 196608 | tf_op jit(solution)/shard_map/psum | solution.py:59
  54.1 687.8 %collective-permute-start.1 = (bf16[96,3072]{1,0:T(8,128)(2,1)}, bf16[96,3072]{1,0:T(8,128)(2,1)}, u32[]{:S(2)}, u32[]{:S(2)}) collective-permute-start(bf16[96,3072]{1,0:T(8,128)(2,1)} %fusion.11), channel_id=1, source_target_pairs={{1,0},{2,1},{3,2},{5,4},{6,5},{7,6},{9,8},{10,9},{11,10},{13,12},{... | collective-permute-start | bytes 1769480 | tf_op jit(solution)/shard_map/ppermute | solution.py:12
  424.2 1.7 copy-start.1
  440.7 301.2 %collective-permute-start = (bf16[96,3072]{1,0:T(8,128)(2,1)}, bf16[96,3072]{1,0:T(8,128)(2,1)}, u32[]{:S(2)}, u32[]{:S(2)}) collective-permute-start(bf16[96,3072]{1,0:T(8,128)(2,1)} %fusion.8), channel_id=1, source_target_pairs={{1,0},{2,1},{3,2},{5,4},{6,5},{7,6},{9,8},{10,9},{11,10},{13,12},{... | collective-permute-start | bytes 1769480 | tf_op jit(solution)/shard_map/ppermute | solution.py:12
Sparse Core Ops, SparseCore 0:
  40.7 320.5 all-reduce.2
  427.5 312.7 all-reduce.4
where the time goes:
time: 753 us; the launch traced here: 752 us
  waiting for transfers between devices  604 us (80%)
  other arithmetic  61.9 us (8%)
  matrix products  60.1 us (8%)
  between operations  19.6 us (3%)
    psum x1, waiting for transfers between devices, per_device(): left_factor = lax.psum(partial_value, 'dp') / replicas  306 us
    psum x1, waiting for transfers between devices, per_device(): right_factor = lax.psum(right_partial, 'dp') / replicas  298 us
    dot_general x5, matrix products, contract(): lax.dot_general(left, right, (((1,), (1,)), ((), ())), preferred_element_...  55.7 us
    reduce_sum x9, other arithmetic, orthonormal(): column = column - jnp.sum(earlier * column) * earlier  28.1 us
    mul x2, other arithmetic, orthonormal(): column = column * lax.rsqrt(jnp.sum(column * column) + 1e-06)  18 us
  transfers between devices with their start and end apart: 6, of which 2 were waited for; matrix products, arithmetic and copies ran while one was open for 14% of the time, Pallas kernels for 0%

commit v1 on v0

v1 whole, which is shorter than its diff:
```python
import functools

import jax
import jax.numpy as jnp
from jax import lax
from jax.experimental import pallas as pl
from jax.experimental.pallas import tpu as pltpu
from jax.sharding import PartitionSpec as P

TOKENS = 384
D_IN = 3072
D_OUT = 3072
RANK = 8
REPLICAS = 32
SECTIONS = 4
ROW_PARTS = 3
CHUNK = 512
PARTS = ((512, 512), (1024, 0), (1024, 0))

VMEM = pltpu.VMEM
F32 = jnp.float32
BF16 = jnp.bfloat16

NT = (((1,), (1,)), ((), ()))
NN = (((1,), (0,)), ((), ()))


def stacked(value):
    high = value.astype(BF16)
    rest = value - high.astype(F32)
    middle = rest.astype(BF16)
    low = (rest - middle.astype(F32)).astype(BF16)
    return jnp.concatenate([high, middle, low], axis=0)


def folded(value):
    return value[:RANK] + (value[RANK : 2 * RANK] + value[2 * RANK :])


def in_vmem(value):
    return pltpu.with_memory_space_constraint(value, VMEM)


def in_hbm(value):
    return pltpu.with_memory_space_constraint(value, pltpu.HBM)


def whole():
    return pl.BlockSpec(memory_space=VMEM)


def anywhere():
    return pl.BlockSpec(memory_space=pl.ANY)


def first_kernel(
    warm_hbm, grads_hbm, inputs_hbm, weight_hbm,
    partial_ref, grads_ref, inputs_ref, ahead_ref, warm_ref, sems,
):
    rows = TOKENS // ROW_PARTS
    warm_copy = pltpu.make_async_copy(warm_hbm, warm_ref, sems.at[0])
    warm_copy.start()
    copies = []
    for part in range(ROW_PARTS):
        span = pl.ds(part * rows, rows)
        copies.append(
            (
                pltpu.make_async_copy(
                    grads_hbm.at[span], grads_ref.at[span], sems.at[2 + 2 * part]
                ),
                pltpu.make_async_copy(
                    inputs_hbm.at[span], inputs_ref.at[span], sems.at[3 + 2 * part]
                ),
            )
        )
    for pair in copies:
        for copy in pair:
            copy.start()
    ahead_copy = pltpu.make_async_copy(weight_hbm.at[pl.ds(0, PARTS[0][0])], ahead_ref, sems.at[1])
    ahead_copy.start()
    warm_copy.wait()
    total = None
    for part in range(ROW_PARTS):
        span = slice(part * rows, (part + 1) * rows)
        copies[part][0].wait()
        projected = stacked(
            lax.dot_general(warm_ref[...], grads_ref[span, :], NT, preferred_element_type=F32)
        )
        copies[part][1].wait()
        term = lax.dot_general(
            projected, inputs_ref[span, :], NN, preferred_element_type=F32
        )
        total = term if total is None else total + term
    partial_ref[...] = folded(total)
    ahead_copy.wait()


def first_products(warm, grads, inputs, weight):
    return pl.pallas_call(
        first_kernel,
        out_shape=(
            VMEM((RANK, D_IN), F32),
            VMEM((TOKENS, D_OUT), BF16),
            VMEM((TOKENS, D_IN), BF16),
            VMEM((PARTS[0][0], D_OUT), BF16),
        ),
        in_specs=[anywhere()] * 4,
        out_specs=(whole(),) * 4,
        scratch_shapes=[
            VMEM((RANK, D_OUT), BF16),
            pltpu.SemaphoreType.DMA((2 + 2 * ROW_PARTS,)),
        ],
        compiler_params=pltpu.CompilerParams(vmem_limit_bytes=16 * 2**20),
        cost_estimate=pl.CostEstimate(
            flops=2 * 64 * TOKENS * D_IN, bytes_accessed=2 * TOKENS * D_IN * 2, transcendentals=0
        ),
        name="first_products",
    )(in_hbm(warm), in_hbm(grads), in_hbm(inputs), in_hbm(weight))


def second_kernel(own_ref, a_ref, b_ref, c_ref, grads_ref, inputs_ref, sum_ref, partial_ref):
    total = (own_ref[...] + a_ref[...]) + (b_ref[...] + c_ref[...])
    sum_ref[...] = total
    backward = folded(
        lax.dot_general(stacked(total), inputs_ref[...], NT, preferred_element_type=F32)
    )
    partial_ref[...] = folded(
        lax.dot_general(stacked(backward), grads_ref[...], NN, preferred_element_type=F32)
    )


def second_products(pieces, grads, inputs):
    return pl.pallas_call(
        second_kernel,
        out_shape=(VMEM((RANK, D_IN), F32), VMEM((RANK, D_OUT), F32)),
        in_specs=[whole()] * 6,
        out_specs=(whole(), whole()),
        compiler_params=pltpu.CompilerParams(vmem_limit_bytes=16 * 2**20),
        cost_estimate=pl.CostEstimate(
            flops=2 * 64 * TOKENS * D_IN, bytes_accessed=RANK * D_IN * 24, transcendentals=0
        ),
        name="second_products",
    )(*[in_vmem(piece) for piece in pieces], in_vmem(grads), in_vmem(inputs))


def gram_schmidt_kernel(sum_ref, left_ref, steps_ref):
    rows = sum_ref[...] * (1.0 / REPLICAS)
    left_ref[...] = rows
    place = lax.broadcasted_iota(jnp.int32, (RANK, 1), 0)
    lane = lax.broadcasted_iota(jnp.int32, (RANK, 128), 1)
    steps = (lax.broadcasted_iota(jnp.int32, (RANK, 128), 0) == lane).astype(F32)
    for rank in range(RANK):
        row = rows[rank : rank + 1]
        step = steps[rank : rank + 1]
        scale = lax.rsqrt(jnp.sum(row * row, axis=1, keepdims=True) + 1e-06)
        row = row * scale
        step = step * scale
        along = jnp.sum(rows * row, axis=1, keepdims=True)
        along = jnp.where(place > rank, along, 0.0)
        rows = rows - along * row
        steps = jnp.where(place == rank, step, steps - along * step)
    steps_ref[...] = steps


def gram_schmidt(total):
    return pl.pallas_call(
        gram_schmidt_kernel,
        out_shape=(
            jax.ShapeDtypeStruct((RANK, D_IN), F32),
            VMEM((RANK, 128), F32),
        ),
        in_specs=[whole()],
        out_specs=(whole(), whole()),
        compiler_params=pltpu.CompilerParams(vmem_limit_bytes=8 * 2**20),
        cost_estimate=pl.CostEstimate(
            flops=64 * RANK * D_IN, bytes_accessed=RANK * D_IN * 8, transcendentals=RANK
        ),
        name="gram_schmidt",
    )(in_vmem(total))


def last_kernel(own_ref, other_ref, steps_ref, right_ref):
    total = (own_ref[...] + other_ref[...]) * (1.0 / REPLICAS**2)
    steps = steps_ref[...]
    result = steps[:, :1] * total[:1]
    for rank in range(1, RANK):
        result = result + steps[:, rank : rank + 1] * total[rank : rank + 1]
    right_ref[...] = result


def last_step(own, other, steps):
    return pl.pallas_call(
        last_kernel,
        out_shape=jax.ShapeDtypeStruct((RANK, D_OUT), F32),
        in_specs=[whole()] * 3,
        out_specs=whole(),
        compiler_params=pltpu.CompilerParams(vmem_limit_bytes=8 * 2**20),
        name="last_step",
    )(in_vmem(own), in_vmem(other), in_vmem(steps))


def product_kernel(base, sizes, ahead, grads_ref, held_ref, weight_hbm, out_ref, *refs):
    held, streamed = sizes
    if ahead:
        ahead_ref, refs = refs[0], refs[1:]
    sems = refs[-1]
    if streamed:
        block_ref = refs[0]
        stream = pltpu.make_async_copy(
            weight_hbm.at[pl.ds(base + held, streamed)], block_ref, sems.at[0]
        )
        stream.start()
    if ahead:
        following = pltpu.make_async_copy(
            weight_hbm.at[pl.ds(base + held + streamed, ahead)], ahead_ref, sems.at[1]
        )
        following.start()

    def product(block_ref, rows, column):
        for row in range(0, rows, CHUNK):
            out_ref[:, column + row : column + row + CHUNK] = lax.dot_general(
                grads_ref[...], block_ref[row : row + CHUNK, :], NT, preferred_element_type=F32
            ).astype(BF16)

    product(held_ref, held, 0)
    if streamed:
        stream.wait()
        product(block_ref, streamed, held)
    if ahead:
        following.wait()


def product_part(grads, held, weight, part):
    sizes = PARTS[part]
    ahead = PARTS[part + 1][0] if part + 1 < len(PARTS) else 0
    base = sum(sum(earlier) for earlier in PARTS[:part])
    out_shape = [VMEM((TOKENS, sum(sizes)), BF16)]
    if ahead:
        out_shape.append(VMEM((ahead, D_OUT), BF16))
    scratch = [pltpu.SemaphoreType.DMA((2,))]
    if sizes[1]:
        scratch.insert(0, VMEM((sizes[1], D_OUT), BF16))
    return pl.pallas_call(
        functools.partial(product_kernel, base, sizes, ahead),
        out_shape=out_shape,
        in_specs=[whole(), whole(), anywhere()],
        out_specs=[whole()] * len(out_shape),
        scratch_shapes=scratch,
        compiler_params=pltpu.CompilerParams(vmem_limit_bytes=24 * 2**20),
        cost_estimate=pl.CostEstimate(
            flops=2 * TOKENS * D_OUT * sum(sizes),
            bytes_accessed=sum(sizes) * D_OUT * 2,
            transcendentals=0,
        ),
        name="product_part",
    )(in_vmem(grads), in_vmem(held), in_hbm(weight))


def store_kernel(*refs):
    *pieces, out_hbm, zeros_ref, sems = refs

    def moved(sources):
        base = 0
        copies = []
        for place, source in enumerate(sources):
            width = source.shape[1]
            copies.append(
                pltpu.make_async_copy(source, out_hbm.at[:, pl.ds(base, width)], sems.at[place])
            )
            base += width
        for copy in copies:
            copy.start()
        for copy in copies:
            copy.wait()

    last = lax.axis_index("section") == SECTIONS - 1

    @pl.when(last)
    def _():
        zeros_ref[...] = jnp.zeros_like(zeros_ref)
        moved([zeros_ref] * (D_IN // CHUNK))

    @pl.when(jnp.logical_not(last))
    def _():
        moved(pieces)


def stored(pieces):
    return pl.pallas_call(
        store_kernel,
        out_shape=jax.ShapeDtypeStruct((TOKENS, D_IN), BF16),
        in_specs=[whole()] * len(pieces),
        out_specs=anywhere(),
        scratch_shapes=[
            VMEM((TOKENS, CHUNK), BF16),
            pltpu.SemaphoreType.DMA((D_IN // CHUNK,)),
        ],
        compiler_params=pltpu.CompilerParams(vmem_limit_bytes=8 * 2**20),
        cost_estimate=pl.CostEstimate(
            flops=0, bytes_accessed=4 * TOKENS * D_IN, transcendentals=0
        ),
        name="store",
    )(*[in_vmem(piece) for piece in pieces])


def replica(y, x, z):
    return (y % 4) * 8 + (x % 2) * 4 + z % 4


def moves(dy, dx, dz):
    return [
        (replica(y, x, z), replica(y + dy, x + dx, z + dz))
        for y in range(4)
        for x in range(2)
        for z in range(4)
    ]


X_ROUND = [moves(0, 1, 0)]
Y_ROUND = [moves(k, 0, 0) for k in (1, 3, 2)]
Z_ROUND = [moves(0, 0, k) for k in (1, 3, 2)]


def sent(value, pattern):
    return [lax.ppermute(value, "dp", pairs) for pairs in pattern]


def tied(*values):
    return lax.optimization_barrier(values)


def handed(piece):
    return lax.ppermute(piece, "section", [(1, 0), (2, 1), (3, 2), (0, 3)])


def per_device(section_inputs, weights, output_grads, warm_start):
    weight = weights[0]
    value, grads, inputs, held = first_products(
        warm_start[0], output_grads[0], section_inputs[0], weight
    )

    arrivals = sent(value, X_ROUND)
    piece, held = product_part(grads, held, weight, 0)
    first = handed(piece)
    value = value + arrivals[0]

    value, held = tied(value, held)
    arrivals = sent(value, Y_ROUND)
    piece, held = product_part(grads, held, weight, 1)
    second = handed(piece)
    value = (value + arrivals[0]) + (arrivals[1] + arrivals[2])

    value, held = tied(value, held)
    arrivals = sent(value, Z_ROUND)
    (piece,) = product_part(grads, held, weight, 2)
    third = handed(piece)
    *pieces, first, _ = tied(value, *arrivals, first, piece)
    total, value = second_products(pieces, grads, inputs)

    arrivals = sent(value, Z_ROUND)
    tied_total, _ = tied(total, value)
    left_factor, steps = gram_schmidt(tied_total)
    value = (value + arrivals[0]) + (arrivals[1] + arrivals[2])
    value, steps, second = tied(value, steps, second)
    arrivals = sent(value, Y_ROUND)
    value = (value + arrivals[0]) + (arrivals[1] + arrivals[2])
    value, first, second, third = tied(value, first, second, third)
    arrivals = sent(value, X_ROUND)
    arrived = stored([first, second, third])
    right_factor = last_step(value, arrivals[0], steps)
    return (arrived[None], left_factor[None], right_factor[None])


def solution(mesh):
    return jax.shard_map(
        per_device,
        mesh=mesh,
        in_specs=(
            P("section", "dp", None),
            P("section", None, None),
            P("section", "dp", None),
            P("section", None, None),
        ),
        out_specs=(P("section", "dp", None), P("section", None, None), P("section", None, None)),
        check_vma=False,
    )
```

time: 753 us -> 58.4 us (0.08)
  waiting for transfers between devices: 604 us -> 15.6 us
  other arithmetic: 61.9 us -> 0.08 us
  matrix products: 60.1 us -> 0 us
  between operations: 19.6 us -> 0.76 us
  starting transfers between devices: 5.51 us -> 23.7 us
  Pallas kernels: 0 us -> 18.1 us
    psum x2 -> x0, waiting for transfers between devices: 604 us -> none  [the longest x1 306 us: per_device(): left_factor = lax.psum(partial_value, 'dp') / replicas]
    dot_general x11 -> x0, matrix products: 60.1 us -> none  [the longest x5 55.7 us: contract(): lax.dot_general(left, right, (((1,), (1,)), ((), ())), preferred_element_...]
    reduce_sum x14 -> x0, other arithmetic: 37 us -> none  [the longest x9 28.1 us: orthonormal(): column = column - jnp.sum(earlier * column) * earlier]
    ppermute x4 -> x17, starting transfers between devices: 5.25 us -> 23.7 us  [the longest x14 23.5 us: sent(): return [lax.ppermute(value, 'dp', pairs) for pairs in pattern]]
    pallas_call x0 -> x8, Pallas kernels: none -> 18.1 us  [the longest x3 9.21 us: product_part(): pl.pallas_call(functools.partial(product_kernel, base, sizes, ahead), out...]
    mul x2 -> x0, other arithmetic: 18 us -> none  [orthonormal(): column = column * lax.rsqrt(jnp.sum(column * column) + 1e-06)]
    ppermute x4 -> x17, waiting for transfers between devices: 0.01 us -> 15.6 us  [the longest x14 15.6 us: sent(): return [lax.ppermute(value, 'dp', pairs) for pairs in pattern]]
  transfers between devices with their start and end apart: 6 -> 17, of which waited for: 2 -> 9; matrix products, arithmetic and copies ran while one was open for 14% -> 0% of each run, Pallas kernels for 0% -> 24%
where the time goes in v1:
time: 58.4 us; the launch traced here: 58.2 us
  starting transfers between devices  23.7 us (41%)
  Pallas kernels  18.1 us (31%)
  waiting for transfers between devices  15.6 us (27%)
  between operations  0.76 us (1%)
    ppermute x14, starting transfers between devices, sent(): return [lax.ppermute(value, 'dp', pairs) for pairs in pattern]  23.5 us
    ppermute x14, waiting for transfers between devices, sent(): return [lax.ppermute(value, 'dp', pairs) for pairs in pattern]  15.6 us
    pallas_call x3, Pallas kernels, product_part(): pl.pallas_call(functools.partial(product_kernel, base, sizes, ahead), out...  9.21 us
    pallas_call x1, Pallas kernels, first_products(): pl.pallas_call(first_kernel, out_shape=(VMEM((RANK, D_IN), F32), VMEM((TO...  3.43 us
    pallas_call x1, Pallas kernels, gram_schmidt(): pl.pallas_call(gram_schmidt_kernel, out_shape=(jax.ShapeDtypeStruct((RANK...  1.6 us
    pallas_call x1, Pallas kernels, second_products(): pl.pallas_call(second_kernel, out_shape=(VMEM((RANK, D_IN), F32), VMEM((R...  1.59 us
    pallas_call x1, Pallas kernels, stored(): pl.pallas_call(store_kernel, out_shape=jax.ShapeDtypeStruct((TOKENS, D_IN...  1.45 us
  transfers between devices with their start and end apart: 17, of which 9 were waited for; matrix products, arithmetic and copies ran while one was open for 0% of the time, Pallas kernels for 24%

profile of v1, /device:TPU:0, one launch (start us, length us, event | category | flops | bytes accessed | tf_op | source)
XLA Modules:
  0.0 58.2 jit_solution(15574502556546743608)
XLA Ops:
  0.6 3.4 %first_products.1 = (f32[8,3072]{1,0:T(8,128)S(1)}, bf16[384,3072]{1,0:T(8,128)(2,1)S(1)}, bf16[384,3072]{1,0:T(8,128)(2,1)S(1)}, bf16[512,3072]{1,0:T(8,128)(2,1)S(1)}) custom-call(bf16[8,3072]{1,0:T(8,128)(2,1)} %bitcast.15, bf16[384,3072]{1,0:T(8,128)(2,1)} %bitcast.11, bf16[384,3072]{1,0:T(8,128)(2,1)} %bitcast.12, bf16[3072,3072]{1,0:T(8,128)(2,1)} %bitcast.7), custom_call_target="tpu_custom_call" | custom-call | flops 150994944 | bytes 4718592 | tf_op jit(solution)/shard_map/first_products/pallas_call | solution.py:99
  4.1 3.2 %collective-permute-start = (f32[8,3072]{1,0:T(8,128)S(1)}, f32[8,3072]{1,0:T(8,128)S(1)}, u32[]{:S(2)}, u32[]{:S(2)}) collective-permute-start(f32[8,3072]{1,0:T(8,128)S(1)} %get-tuple-element.32), channel_id=1, source_target_pairs={{0,16},{4,20},{8,24},{12,28},{16,0},{20,4},{24,8},{28,12},{32,48},... | collective-permute-start | bytes 294920 | tf_op jit(solution)/shard_map/ppermute | solution.py:325
  7.3 3.8 %product_part.3 = (bf16[384,1024]{1,0:T(8,128)(2,1)S(1)}, bf16[1024,3072]{1,0:T(8,128)(2,1)S(1)}) custom-call(bf16[384,3072]{1,0:T(8,128)(2,1)S(1)} %get-tuple-element.33.grads_ref, bf16[512,3072]{1,0:T(8,128)(2,1)S(1)} %get-tuple-element.34.held_ref, bf16[3072,3072]{1,0:T(8,128)(2,1)} %bitcast.8), custom_call_target="tpu_custom_call" | custom-call | flops 2415919104 | bytes 6291456 | tf_op jit(solution)/shard_map/product_part/pallas_call | solution.py:243
  11.0 0.1 collective-permute-start.7
  11.1 0.0 collective-permute-done
  11.1 3.3 %collective-permute-start.3 = (f32[8,3072]{1,0:T(8,128)S(1)}, f32[8,3072]{1,0:T(8,128)S(1)}, u32[]{:S(2)}, u32[]{:S(2)}) collective-permute-start(f32[8,3072]{1,0:T(8,128)S(1)} %add.30), channel_id=1, source_target_pairs={{0,64},{4,68},{8,72},{12,76},{16,80},{20,84},{24,88},{28,92},{32,9... | collective-permute-start | bytes 294920 | tf_op jit(solution)/shard_map/ppermute | solution.py:325
  14.4 1.1 %collective-permute-start.2 = (f32[8,3072]{1,0:T(8,128)S(1)}, f32[8,3072]{1,0:T(8,128)S(1)}, u32[]{:S(2)}, u32[]{:S(2)}) collective-permute-start(f32[8,3072]{1,0:T(8,128)S(1)} %add.30), channel_id=1, source_target_pairs={{0,96},{4,100},{8,104},{12,108},{16,112},{20,116},{24,120},{28,124... | collective-permute-start | bytes 294920 | tf_op jit(solution)/shard_map/ppermute | solution.py:325
  15.5 1.0 %collective-permute-start.1 = (f32[8,3072]{1,0:T(8,128)S(1)}, f32[8,3072]{1,0:T(8,128)S(1)}, u32[]{:S(2)}, u32[]{:S(2)}) collective-permute-start(f32[8,3072]{1,0:T(8,128)S(1)} %add.30), channel_id=1, source_target_pairs={{0,32},{4,36},{8,40},{12,44},{16,48},{20,52},{24,56},{28,60},{32,6... | collective-permute-start | bytes 294920 | tf_op jit(solution)/shard_map/ppermute | solution.py:325
  16.4 2.8 %product_part.4 = (bf16[384,1024]{1,0:T(8,128)(2,1)S(1)}, bf16[1024,3072]{1,0:T(8,128)(2,1)S(1)}) custom-call(bf16[384,3072]{1,0:T(8,128)(2,1)S(1)} %get-tuple-element.33.grads_ref, bf16[1024,3072]{1,0:T(8,128)(2,1)S(1)} %get-tuple-element.37.held_ref, bf16[3072,3072]{1,0:T(8,128)(2,1)} %bitcast.9), custom_call_target="tpu_custom_call" | custom-call | flops 2415919104 | bytes 6291456 | tf_op jit(solution)/shard_map/product_part/pallas_call | solution.py:243
  19.2 0.1 collective-permute-start.11
  19.3 0.0 collective-permute-done.3
  19.3 1.0 %collective-permute-done.2 = f32[8,3072]{1,0:T(8,128)S(1)} collective-permute-done((f32[8,3072]{1,0:T(8,128)S(1)}, f32[8,3072]{1,0:T(8,128)S(1)}, u32[]{:S(2)}, u32[]{:S(2)}) %collective-permute-start.2) | collective-permute-done | bytes 98336 | tf_op jit(solution)/shard_map/ppermute | solution.py:325
  20.4 0.9 %collective-permute-done.1 = f32[8,3072]{1,0:T(8,128)S(1)} collective-permute-done((f32[8,3072]{1,0:T(8,128)S(1)}, f32[8,3072]{1,0:T(8,128)S(1)}, u32[]{:S(2)}, u32[]{:S(2)}) %collective-permute-start.1) | collective-permute-done | bytes 98336 | tf_op jit(solution)/shard_map/ppermute | solution.py:325
  21.3 4.0 %collective-permute-start.6 = (f32[8,3072]{1,0:T(8,128)S(1)}, f32[8,3072]{1,0:T(8,128)S(1)}, u32[]{:S(2)}, u32[]{:S(2)}) collective-permute-start(f32[8,3072]{1,0:T(8,128)S(1)} %add_add_fusion.2.own_ref), channel_id=1, source_target_pairs={{0,8},{4,12},{8,0},{12,4},{16,24},{20,28},{24,16},{28,20},{32,40},... | collective-permute-start | bytes 294920 | tf_op jit(solution)/shard_map/ppermute | solution.py:325
  25.3 0.7 %collective-permute-start.5 = (f32[8,3072]{1,0:T(8,128)S(1)}, f32[8,3072]{1,0:T(8,128)S(1)}, u32[]{:S(2)}, u32[]{:S(2)}) collective-permute-start(f32[8,3072]{1,0:T(8,128)S(1)} %add_add_fusion.2.own_ref), channel_id=1, source_target_pairs={{0,12},{4,0},{8,4},{12,8},{16,28},{20,16},{24,20},{28,24},{32,44},... | collective-permute-start | bytes 294920 | tf_op jit(solution)/shard_map/ppermute | solution.py:325
  26.0 1.3 %collective-permute-start.4 = (f32[8,3072]{1,0:T(8,128)S(1)}, f32[8,3072]{1,0:T(8,128)S(1)}, u32[]{:S(2)}, u32[]{:S(2)}) collective-permute-start(f32[8,3072]{1,0:T(8,128)S(1)} %add_add_fusion.2.own_ref), channel_id=1, source_target_pairs={{0,4},{4,8},{8,12},{12,0},{16,20},{20,24},{24,28},{28,16},{32,36},... | collective-permute-start | bytes 294920 | tf_op jit(solution)/shard_map/ppermute | solution.py:325
  27.3 2.6 %product_part.5 = bf16[384,1024]{1,0:T(8,128)(2,1)S(1)} custom-call(bf16[384,3072]{1,0:T(8,128)(2,1)S(1)} %get-tuple-element.33.grads_ref, bf16[1024,3072]{1,0:T(8,128)(2,1)S(1)} %get-tuple-element.41.held_ref, bf16[3072,3072]{1,0:T(8,128)(2,1)} %bitcast.10), custom_call_target="tpu_custom_call" | custom-call | flops 2415919104 | bytes 6291456 | tf_op jit(solution)/shard_map/product_part/pallas_call | solution.py:243
  30.0 0.0 collective-permute-done.6.c_ref
  30.0 0.0 collective-permute-done.5.b_ref
  30.0 1.8 %collective-permute-done.4.a_ref = f32[8,3072]{1,0:T(8,128)S(1)} collective-permute-done((f32[8,3072]{1,0:T(8,128)S(1)}, f32[8,3072]{1,0:T(8,128)S(1)}, u32[]{:S(2)}, u32[]{:S(2)}) %collective-permute-start.4) | collective-permute-done | bytes 98336 | tf_op jit(solution)/shard_map/ppermute | solution.py:325
  31.8 0.0 collective-permute-done.7.refs_0_
  31.8 1.6 %second_products.1 = (f32[8,3072]{1,0:T(8,128)S(1)}, f32[8,3072]{1,0:T(8,128)S(1)}) custom-call(f32[8,3072]{1,0:T(8,128)S(1)} %add_add_fusion.2.own_ref, f32[8,3072]{1,0:T(8,128)S(1)} %collective-permute-done.4.a_ref, f32[8,3072]{1,0:T(8,128)S(1)} %collective-permute-done.5.b_ref, f32[8,3072]{1,0:T(8,128)S(1)} %collective-permute-done.6.c_ref, ...), custom_call_target="tpu_custom_call" | custom-call | flops 150994944 | bytes 589824 | tf_op jit(solution)/shard_map/second_products/pallas_call | solution.py:133
  33.4 1.2 %collective-permute-start.10 = (f32[8,3072]{1,0:T(8,128)S(1)}, f32[8,3072]{1,0:T(8,128)S(1)}, u32[]{:S(2)}, u32[]{:S(2)}) collective-permute-start(f32[8,3072]{1,0:T(8,128)S(1)} %get-tuple-element.47), channel_id=1, source_target_pairs={{0,8},{4,12},{8,0},{12,4},{16,24},{20,28},{24,16},{28,20},{32,40},... | collective-permute-start | bytes 294920 | tf_op jit(solution)/shard_map/ppermute | solution.py:325
  34.6 1.6 %collective-permute-start.9 = (f32[8,3072]{1,0:T(8,128)S(1)}, f32[8,3072]{1,0:T(8,128)S(1)}, u32[]{:S(2)}, u32[]{:S(2)}) collective-permute-start(f32[8,3072]{1,0:T(8,128)S(1)} %get-tuple-element.47), channel_id=1, source_target_pairs={{0,12},{4,0},{8,4},{12,8},{16,28},{20,16},{24,20},{28,24},{32,44},... | collective-permute-start | bytes 294920 | tf_op jit(solution)/shard_map/ppermute | solution.py:325
  36.3 0.4 collective-permute-start.8
  36.7 0.0 collective-permute-start.15
  36.7 1.6 %gram_schmidt.1 = (f32[8,3072]{1,0:T(8,128)}, f32[8,128]{1,0:T(8,128)S(1)}) custom-call(f32[8,3072]{1,0:T(8,128)S(1)} %get-tuple-element.48.sum_ref), custom_call_target="tpu_custom_call" | custom-call | flops 1572864 | bytes 196608 | tf_op jit(solution)/shard_map/gram_schmidt/pallas_call | solution.py:166
  38.3 1.3 %collective-permute-done.10 = f32[8,3072]{1,0:T(8,128)S(1)} collective-permute-done((f32[8,3072]{1,0:T(8,128)S(1)}, f32[8,3072]{1,0:T(8,128)S(1)}, u32[]{:S(2)}, u32[]{:S(2)}) %collective-permute-start.10) | collective-permute-done | bytes 98336 | tf_op jit(solution)/shard_map/ppermute | solution.py:325
  39.6 0.0 collective-permute-done.9
  39.6 2.5 %collective-permute-done.8 = f32[8,3072]{1,0:T(8,128)S(1)} collective-permute-done((f32[8,3072]{1,0:T(8,128)S(1)}, f32[8,3072]{1,0:T(8,128)S(1)}, u32[]{:S(2)}, u32[]{:S(2)}) %collective-permute-start.8) | collective-permute-done | bytes 98336 | tf_op jit(solution)/shard_map/ppermute | solution.py:325
  42.1 0.0 collective-permute-done.11.refs_1_
  42.1 2.2 %collective-permute-start.14 = (f32[8,3072]{1,0:T(8,128)S(1)}, f32[8,3072]{1,0:T(8,128)S(1)}, u32[]{:S(2)}, u32[]{:S(2)}) collective-permute-start(f32[8,3072]{1,0:T(8,128)S(1)} %add_add_fusion.1), channel_id=1, source_target_pairs={{0,64},{4,68},{8,72},{12,76},{16,80},{20,84},{24,88},{28,92},{32,9... | collective-permute-start | bytes 294920 | tf_op jit(solution)/shard_map/ppermute | solution.py:325
  44.3 1.1 %collective-permute-start.13 = (f32[8,3072]{1,0:T(8,128)S(1)}, f32[8,3072]{1,0:T(8,128)S(1)}, u32[]{:S(2)}, u32[]{:S(2)}) collective-permute-start(f32[8,3072]{1,0:T(8,128)S(1)} %add_add_fusion.1), channel_id=1, source_target_pairs={{0,96},{4,100},{8,104},{12,108},{16,112},{20,116},{24,120},{28,124... | collective-permute-start | bytes 294920 | tf_op jit(solution)/shard_map/ppermute | solution.py:325
  45.4 0.9 %collective-permute-start.12 = (f32[8,3072]{1,0:T(8,128)S(1)}, f32[8,3072]{1,0:T(8,128)S(1)}, u32[]{:S(2)}, u32[]{:S(2)}) collective-permute-start(f32[8,3072]{1,0:T(8,128)S(1)} %add_add_fusion.1), channel_id=1, source_target_pairs={{0,32},{4,36},{8,40},{12,44},{16,48},{20,52},{24,56},{28,60},{32,6... | collective-permute-start | bytes 294920 | tf_op jit(solution)/shard_map/ppermute | solution.py:325
  46.3 2.1 %collective-permute-done.14 = f32[8,3072]{1,0:T(8,128)S(1)} collective-permute-done((f32[8,3072]{1,0:T(8,128)S(1)}, f32[8,3072]{1,0:T(8,128)S(1)}, u32[]{:S(2)}, u32[]{:S(2)}) %collective-permute-start.14) | collective-permute-done | bytes 98336 | tf_op jit(solution)/shard_map/ppermute | solution.py:325
  48.4 0.5 collective-permute-done.13
  48.9 2.3 %collective-permute-done.12 = f32[8,3072]{1,0:T(8,128)S(1)} collective-permute-done((f32[8,3072]{1,0:T(8,128)S(1)}, f32[8,3072]{1,0:T(8,128)S(1)}, u32[]{:S(2)}, u32[]{:S(2)}) %collective-permute-start.12) | collective-permute-done | bytes 98336 | tf_op jit(solution)/shard_map/ppermute | solution.py:325
  51.2 0.0 collective-permute-done.15.refs_2_
  51.2 1.6 %collective-permute-start.16 = (f32[8,3072]{1,0:T(8,128)S(1)}, f32[8,3072]{1,0:T(8,128)S(1)}, u32[]{:S(2)}, u32[]{:S(2)}) collective-permute-start(f32[8,3072]{1,0:T(8,128)S(1)} %add_add_fusion.own_ref), channel_id=1, source_target_pairs={{0,16},{4,20},{8,24},{12,28},{16,0},{20,4},{24,8},{28,12},{32,48},... | collective-permute-start | bytes 294920 | tf_op jit(solution)/shard_map/ppermute | solution.py:325
  52.9 1.4 %store.1 = bf16[384,3072]{1,0:T(8,128)(2,1)} custom-call(bf16[384,1024]{1,0:T(8,128)(2,1)S(1)} %collective-permute-done.7.refs_0_, bf16[384,1024]{1,0:T(8,128)(2,1)S(1)} %collective-permute-done.11.refs_1_, bf16[384,1024]{1,0:T(8,128)(2,1)S(1)} %collective-permute-done.15.refs_2_), custom_call_target="tpu_custom_call" | custom-call | bytes 4718592 | tf_op jit(solution)/shard_map/store/pallas_call | solution.py:289
  54.3 3.1 %collective-permute-done.16.other_ref = f32[8,3072]{1,0:T(8,128)S(1)} collective-permute-done((f32[8,3072]{1,0:T(8,128)S(1)}, f32[8,3072]{1,0:T(8,128)S(1)}, u32[]{:S(2)}, u32[]{:S(2)}) %collective-permute-start.16) | collective-permute-done | bytes 98336 | tf_op jit(solution)/shard_map/ppermute | solution.py:325
  57.4 0.8 %last_step.1 = f32[8,3072]{1,0:T(8,128)} custom-call(f32[8,3072]{1,0:T(8,128)S(1)} %add_add_fusion.own_ref, f32[8,3072]{1,0:T(8,128)S(1)} %collective-permute-done.16.other_ref, f32[8,128]{1,0:T(8,128)S(1)} %get-tuple-element.59.steps_ref), custom_call_target="tpu_custom_call" | custom-call | tf_op jit(solution)/shard_map/last_step/pallas_call | solution.py:192
  (4 shorter events, 0.1 us)
Async XLA Ops:
  4.1 7.0 %collective-permute-start = (f32[8,3072]{1,0:T(8,128)S(1)}, f32[8,3072]{1,0:T(8,128)S(1)}, u32[]{:S(2)}, u32[]{:S(2)}) collective-permute-start(f32[8,3072]{1,0:T(8,128)S(1)} %get-tuple-element.32), channel_id=1, source_target_pairs={{0,16},{4,20},{8,24},{12,28},{16,0},{20,4},{24,8},{28,12},{32,48},... | collective-permute-start | bytes 294920 | tf_op jit(solution)/shard_map/ppermute | solution.py:325
  11.0 20.8 %collective-permute-start.7 = (bf16[384,1024]{1,0:T(8,128)(2,1)S(1)}, bf16[384,1024]{1,0:T(8,128)(2,1)S(1)}, u32[]{:S(2)}, u32[]{:S(2)}) collective-permute-start(bf16[384,1024]{1,0:T(8,128)(2,1)S(1)} %get-tuple-element.40), channel_id=1, source_target_pairs={{1,0},{2,1},{3,2},{0,3},{5,4},{6,5},{7,6},{4,7},{9,8},{10,9},{11,1... | collective-permute-start | bytes 2359304 | tf_op jit(solution)/shard_map/ppermute | solution.py:333
  11.1 8.2 %collective-permute-start.3 = (f32[8,3072]{1,0:T(8,128)S(1)}, f32[8,3072]{1,0:T(8,128)S(1)}, u32[]{:S(2)}, u32[]{:S(2)}) collective-permute-start(f32[8,3072]{1,0:T(8,128)S(1)} %add.30), channel_id=1, source_target_pairs={{0,64},{4,68},{8,72},{12,76},{16,80},{20,84},{24,88},{28,92},{32,9... | collective-permute-start | bytes 294920 | tf_op jit(solution)/shard_map/ppermute | solution.py:325
  14.4 5.9 %collective-permute-start.2 = (f32[8,3072]{1,0:T(8,128)S(1)}, f32[8,3072]{1,0:T(8,128)S(1)}, u32[]{:S(2)}, u32[]{:S(2)}) collective-permute-start(f32[8,3072]{1,0:T(8,128)S(1)} %add.30), channel_id=1, source_target_pairs={{0,96},{4,100},{8,104},{12,108},{16,112},{20,116},{24,120},{28,124... | collective-permute-start | bytes 294920 | tf_op jit(solution)/shard_map/ppermute | solution.py:325
  15.5 5.8 %collective-permute-start.1 = (f32[8,3072]{1,0:T(8,128)S(1)}, f32[8,3072]{1,0:T(8,128)S(1)}, u32[]{:S(2)}, u32[]{:S(2)}) collective-permute-start(f32[8,3072]{1,0:T(8,128)S(1)} %add.30), channel_id=1, source_target_pairs={{0,32},{4,36},{8,40},{12,44},{16,48},{20,52},{24,56},{28,60},{32,6... | collective-permute-start | bytes 294920 | tf_op jit(solution)/shard_map/ppermute | solution.py:325
  19.2 22.9 %collective-permute-start.11 = (bf16[384,1024]{1,0:T(8,128)(2,1)S(1)}, bf16[384,1024]{1,0:T(8,128)(2,1)S(1)}, u32[]{:S(2)}, u32[]{:S(2)}) collective-permute-start(bf16[384,1024]{1,0:T(8,128)(2,1)S(1)} %get-tuple-element.50), channel_id=1, source_target_pairs={{1,0},{2,1},{3,2},{0,3},{5,4},{6,5},{7,6},{4,7},{9,8},{10,9},{11,1... | collective-permute-start | bytes 2359304 | tf_op jit(solution)/shard_map/ppermute | solution.py:333
  21.3 8.6 %collective-permute-start.6 = (f32[8,3072]{1,0:T(8,128)S(1)}, f32[8,3072]{1,0:T(8,128)S(1)}, u32[]{:S(2)}, u32[]{:S(2)}) collective-permute-start(f32[8,3072]{1,0:T(8,128)S(1)} %add_add_fusion.2.own_ref), channel_id=1, source_target_pairs={{0,8},{4,12},{8,0},{12,4},{16,24},{20,28},{24,16},{28,20},{32,40},... | collective-permute-start | bytes 294920 | tf_op jit(solution)/shard_map/ppermute | solution.py:325
  25.3 4.7 %collective-permute-start.5 = (f32[8,3072]{1,0:T(8,128)S(1)}, f32[8,3072]{1,0:T(8,128)S(1)}, u32[]{:S(2)}, u32[]{:S(2)}) collective-permute-start(f32[8,3072]{1,0:T(8,128)S(1)} %add_add_fusion.2.own_ref), channel_id=1, source_target_pairs={{0,12},{4,0},{8,4},{12,8},{16,28},{20,16},{24,20},{28,24},{32,44},... | collective-permute-start | bytes 294920 | tf_op jit(solution)/shard_map/ppermute | solution.py:325
  26.0 5.8 %collective-permute-start.4 = (f32[8,3072]{1,0:T(8,128)S(1)}, f32[8,3072]{1,0:T(8,128)S(1)}, u32[]{:S(2)}, u32[]{:S(2)}) collective-permute-start(f32[8,3072]{1,0:T(8,128)S(1)} %add_add_fusion.2.own_ref), channel_id=1, source_target_pairs={{0,4},{4,8},{8,12},{12,0},{16,20},{20,24},{24,28},{28,16},{32,36},... | collective-permute-start | bytes 294920 | tf_op jit(solution)/shard_map/ppermute | solution.py:325
  33.4 6.2 %collective-permute-start.10 = (f32[8,3072]{1,0:T(8,128)S(1)}, f32[8,3072]{1,0:T(8,128)S(1)}, u32[]{:S(2)}, u32[]{:S(2)}) collective-permute-start(f32[8,3072]{1,0:T(8,128)S(1)} %get-tuple-element.47), channel_id=1, source_target_pairs={{0,8},{4,12},{8,0},{12,4},{16,24},{20,28},{24,16},{28,20},{32,40},... | collective-permute-start | bytes 294920 | tf_op jit(solution)/shard_map/ppermute | solution.py:325
  34.6 5.0 %collective-permute-start.9 = (f32[8,3072]{1,0:T(8,128)S(1)}, f32[8,3072]{1,0:T(8,128)S(1)}, u32[]{:S(2)}, u32[]{:S(2)}) collective-permute-start(f32[8,3072]{1,0:T(8,128)S(1)} %get-tuple-element.47), channel_id=1, source_target_pairs={{0,12},{4,0},{8,4},{12,8},{16,28},{20,16},{24,20},{28,24},{32,44},... | collective-permute-start | bytes 294920 | tf_op jit(solution)/shard_map/ppermute | solution.py:325
  36.3 5.8 %collective-permute-start.8 = (f32[8,3072]{1,0:T(8,128)S(1)}, f32[8,3072]{1,0:T(8,128)S(1)}, u32[]{:S(2)}, u32[]{:S(2)}) collective-permute-start(f32[8,3072]{1,0:T(8,128)S(1)} %get-tuple-element.47), channel_id=1, source_target_pairs={{0,4},{4,8},{8,12},{12,0},{16,20},{20,24},{24,28},{28,16},{32,36},... | collective-permute-start | bytes 294920 | tf_op jit(solution)/shard_map/ppermute | solution.py:325
  36.7 14.6 %collective-permute-start.15 = (bf16[384,1024]{1,0:T(8,128)(2,1)S(1)}, bf16[384,1024]{1,0:T(8,128)(2,1)S(1)}, u32[]{:S(2)}, u32[]{:S(2)}) collective-permute-start(bf16[384,1024]{1,0:T(8,128)(2,1)S(1)} %product_part.5), channel_id=1, source_target_pairs={{1,0},{2,1},{3,2},{0,3},{5,4},{6,5},{7,6},{4,7},{9,8},{10,9},{11,1... | collective-permute-start | bytes 2359304 | tf_op jit(solution)/shard_map/ppermute | solution.py:333
  42.1 6.3 %collective-permute-start.14 = (f32[8,3072]{1,0:T(8,128)S(1)}, f32[8,3072]{1,0:T(8,128)S(1)}, u32[]{:S(2)}, u32[]{:S(2)}) collective-permute-start(f32[8,3072]{1,0:T(8,128)S(1)} %add_add_fusion.1), channel_id=1, source_target_pairs={{0,64},{4,68},{8,72},{12,76},{16,80},{20,84},{24,88},{28,92},{32,9... | collective-permute-start | bytes 294920 | tf_op jit(solution)/shard_map/ppermute | solution.py:325
  44.3 4.6 %collective-permute-start.13 = (f32[8,3072]{1,0:T(8,128)S(1)}, f32[8,3072]{1,0:T(8,128)S(1)}, u32[]{:S(2)}, u32[]{:S(2)}) collective-permute-start(f32[8,3072]{1,0:T(8,128)S(1)} %add_add_fusion.1), channel_id=1, source_target_pairs={{0,96},{4,100},{8,104},{12,108},{16,112},{20,116},{24,120},{28,124... | collective-permute-start | bytes 294920 | tf_op jit(solution)/shard_map/ppermute | solution.py:325
  45.4 5.8 %collective-permute-start.12 = (f32[8,3072]{1,0:T(8,128)S(1)}, f32[8,3072]{1,0:T(8,128)S(1)}, u32[]{:S(2)}, u32[]{:S(2)}) collective-permute-start(f32[8,3072]{1,0:T(8,128)S(1)} %add_add_fusion.1), channel_id=1, source_target_pairs={{0,32},{4,36},{8,40},{12,44},{16,48},{20,52},{24,56},{28,60},{32,6... | collective-permute-start | bytes 294920 | tf_op jit(solution)/shard_map/ppermute | solution.py:325
  51.2 6.2 %collective-permute-start.16 = (f32[8,3072]{1,0:T(8,128)S(1)}, f32[8,3072]{1,0:T(8,128)S(1)}, u32[]{:S(2)}, u32[]{:S(2)}) collective-permute-start(f32[8,3072]{1,0:T(8,128)S(1)} %add_add_fusion.own_ref), channel_id=1, source_target_pairs={{0,16},{4,20},{8,24},{12,28},{16,0},{20,4},{24,8},{28,12},{32,48},... | collective-permute-start | bytes 294920 | tf_op jit(solution)/shard_map/ppermute | solution.py:325

commit v2 on v1

v2 whole, which is shorter than its diff:
```python
import functools

import jax
import jax.numpy as jnp
from jax import lax
from jax.experimental import pallas as pl
from jax.experimental.pallas import tpu as pltpu
from jax.sharding import PartitionSpec as P

TOKENS = 384
D_IN = 3072
D_OUT = 3072
RANK = 8
REPLICAS = 32
SECTIONS = 4
ROW_PARTS = 3
WINDOW = 4
WIRE = jnp.bfloat16
CHUNK = 512
PARTS = ((512, 512), (1024, 0), (1024, 0))

VMEM = pltpu.VMEM
F32 = jnp.float32
BF16 = jnp.bfloat16

NT = (((1,), (1,)), ((), ()))
NN = (((1,), (0,)), ((), ()))


def stacked(value):
    high = value.astype(BF16)
    rest = value - high.astype(F32)
    middle = rest.astype(BF16)
    low = (rest - middle.astype(F32)).astype(BF16)
    return jnp.concatenate([high, middle, low], axis=0)


def folded(value):
    return value[:RANK] + (value[RANK : 2 * RANK] + value[2 * RANK :])


def in_vmem(value):
    return pltpu.with_memory_space_constraint(value, VMEM)


def in_hbm(value):
    return pltpu.with_memory_space_constraint(value, pltpu.HBM)


def whole():
    return pl.BlockSpec(memory_space=VMEM)


def anywhere():
    return pl.BlockSpec(memory_space=pl.ANY)


def first_kernel(
    warm_hbm, grads_hbm, inputs_hbm, weight_hbm, partial_ref, grads_ref, inputs_ref, *refs
):
    ahead = PARTS[0][0]
    if ahead:
        ahead_ref, refs = refs[0], refs[1:]
    warm_ref, sems = refs
    rows = TOKENS // ROW_PARTS
    warm_copy = pltpu.make_async_copy(warm_hbm, warm_ref, sems.at[0])
    warm_copy.start()
    copies = []
    for part in range(ROW_PARTS):
        span = pl.ds(part * rows, rows)
        copies.append(
            (
                pltpu.make_async_copy(
                    grads_hbm.at[span], grads_ref.at[span], sems.at[2 + 2 * part]
                ),
                pltpu.make_async_copy(
                    inputs_hbm.at[span], inputs_ref.at[span], sems.at[3 + 2 * part]
                ),
            )
        )
    if ahead:
        ahead_copy = pltpu.make_async_copy(
            weight_hbm.at[pl.ds(0, ahead)], ahead_ref, sems.at[1]
        )

    def start(part):
        if part < ROW_PARTS:
            for copy in copies[part]:
                copy.start()
        elif ahead and part == ROW_PARTS:
            ahead_copy.start()

    for part in range(WINDOW):
        start(part)
    warm_copy.wait()
    total = None
    for part in range(ROW_PARTS):
        span = slice(part * rows, (part + 1) * rows)
        copies[part][0].wait()
        start(part + WINDOW)
        projected = stacked(
            lax.dot_general(warm_ref[...], grads_ref[span, :], NT, preferred_element_type=F32)
        )
        copies[part][1].wait()
        term = lax.dot_general(
            projected, inputs_ref[span, :], NN, preferred_element_type=F32
        )
        total = term if total is None else total + term
    partial_ref[...] = folded(total)
    if ahead:
        ahead_copy.wait()


def first_products(warm, grads, inputs, weight):
    ahead = PARTS[0][0]
    out_shape = [
        VMEM((RANK, D_IN), F32),
        VMEM((TOKENS, D_OUT), BF16),
        VMEM((TOKENS, D_IN), BF16),
    ]
    if ahead:
        out_shape.append(VMEM((ahead, D_OUT), BF16))
    results = pl.pallas_call(
        first_kernel,
        out_shape=out_shape,
        in_specs=[anywhere()] * 4,
        out_specs=[whole()] * len(out_shape),
        scratch_shapes=[
            VMEM((RANK, D_OUT), BF16),
            pltpu.SemaphoreType.DMA((2 + 2 * ROW_PARTS,)),
        ],
        compiler_params=pltpu.CompilerParams(vmem_limit_bytes=16 * 2**20),
        cost_estimate=pl.CostEstimate(
            flops=2 * 64 * TOKENS * D_IN, bytes_accessed=2 * TOKENS * D_IN * 2, transcendentals=0
        ),
        name="first_products",
    )(in_hbm(warm), in_hbm(grads), in_hbm(inputs), in_hbm(weight))
    return list(results) if ahead else [*results, None]


def gram_schmidt_steps(rows):
    place = lax.broadcasted_iota(jnp.int32, (RANK, 1), 0)
    lane = lax.broadcasted_iota(jnp.int32, (RANK, 128), 1)
    steps = (lax.broadcasted_iota(jnp.int32, (RANK, 128), 0) == lane).astype(F32)
    for rank in range(RANK):
        row = rows[rank : rank + 1]
        step = steps[rank : rank + 1]
        scale = lax.rsqrt(jnp.sum(row * row, axis=1, keepdims=True) + 1e-06)
        row = row * scale
        step = step * scale
        along = jnp.sum(rows * row, axis=1, keepdims=True)
        along = jnp.where(place > rank, along, 0.0)
        rows = rows - along * row
        steps = jnp.where(place == rank, step, steps - along * step)
    return steps


def applied(steps, value):
    result = steps[:, :1] * value[:1]
    for rank in range(1, RANK):
        result = result + steps[:, rank : rank + 1] * value[rank : rank + 1]
    return result


def second_kernel(own_ref, a_ref, b_ref, c_ref, grads_ref, inputs_ref, left_ref, partial_ref):
    total = (own_ref[...] + a_ref[...]) + (b_ref[...] + c_ref[...])
    total = total * (1.0 / REPLICAS)
    left_ref[...] = total
    steps = gram_schmidt_steps(total)
    backward = folded(
        lax.dot_general(stacked(total), inputs_ref[...], NT, preferred_element_type=F32)
    )
    partial_value = folded(
        lax.dot_general(stacked(backward), grads_ref[...], NN, preferred_element_type=F32)
    )
    partial_ref[...] = (applied(steps, partial_value) * (1.0 / REPLICAS)).astype(
        partial_ref.dtype
    )


def second_products(pieces, grads, inputs):
    return pl.pallas_call(
        second_kernel,
        out_shape=(VMEM((RANK, D_IN), F32), VMEM((RANK, D_OUT), WIRE)),
        in_specs=[whole()] * 6,
        out_specs=(whole(), whole()),
        compiler_params=pltpu.CompilerParams(vmem_limit_bytes=16 * 2**20),
        cost_estimate=pl.CostEstimate(
            flops=2 * 64 * TOKENS * D_IN, bytes_accessed=RANK * D_IN * 24, transcendentals=0
        ),
        name="second_products",
    )(*[in_vmem(piece) for piece in pieces], in_vmem(grads), in_vmem(inputs))


def left_kernel(left_ref, out_hbm, sem):
    copy = pltpu.make_async_copy(left_ref, out_hbm, sem)
    copy.start()
    copy.wait()


def left_stored(left):
    return pl.pallas_call(
        left_kernel,
        out_shape=jax.ShapeDtypeStruct((RANK, D_IN), F32),
        in_specs=[whole()],
        out_specs=anywhere(),
        scratch_shapes=[pltpu.SemaphoreType.DMA],
        compiler_params=pltpu.CompilerParams(vmem_limit_bytes=2 * 2**20),
        name="left_stored",
    )(in_vmem(left))


def widened(*values):
    values = [value.astype(F32) for value in values]
    return functools.reduce(lambda left, right: left + right, values)


def product_kernel(base, sizes, ahead, grads_ref, *refs):
    held, streamed = sizes
    if held:
        held_ref, refs = refs[0], refs[1:]
    weight_hbm, out_ref, *refs = refs
    if ahead:
        ahead_ref, refs = refs[0], refs[1:]
    sems = refs[-1]
    streams = []
    for row in range(0, streamed, CHUNK):
        streams.append(
            pltpu.make_async_copy(
                weight_hbm.at[pl.ds(base + held + row, CHUNK)],
                refs[0].at[pl.ds(row, CHUNK)],
                sems.at[1 + row // CHUNK],
            )
        )
    for stream in streams:
        stream.start()
    if ahead:
        following = pltpu.make_async_copy(
            weight_hbm.at[pl.ds(base + held + streamed, ahead)], ahead_ref, sems.at[0]
        )
        following.start()

    def product(block_ref, row, column):
        out_ref[:, column : column + CHUNK] = lax.dot_general(
            grads_ref[...], block_ref[row : row + CHUNK, :], NT, preferred_element_type=F32
        ).astype(BF16)

    for row in range(0, held, CHUNK):
        product(held_ref, row, row)
    for row in range(0, streamed, CHUNK):
        streams[row // CHUNK].wait()
        product(refs[0], row, held + row)
    if ahead:
        following.wait()


def product_part(grads, held, weight, part):
    sizes = PARTS[part]
    ahead = PARTS[part + 1][0] if part + 1 < len(PARTS) else 0
    base = sum(sum(earlier) for earlier in PARTS[:part])
    operands = [in_vmem(grads)]
    if sizes[0]:
        operands.append(in_vmem(held))
    operands.append(in_hbm(weight))
    out_shape = [VMEM((TOKENS, sum(sizes)), BF16)]
    if ahead:
        out_shape.append(VMEM((ahead, D_OUT), BF16))
    scratch = [pltpu.SemaphoreType.DMA((1 + D_IN // CHUNK,))]
    if sizes[1]:
        scratch.insert(0, VMEM((sizes[1], D_OUT), BF16))
    return pl.pallas_call(
        functools.partial(product_kernel, base, sizes, ahead),
        out_shape=out_shape,
        in_specs=[whole()] * (len(operands) - 1) + [anywhere()],
        out_specs=[whole()] * len(out_shape),
        scratch_shapes=scratch,
        compiler_params=pltpu.CompilerParams(vmem_limit_bytes=32 * 2**20),
        cost_estimate=pl.CostEstimate(
            flops=2 * TOKENS * D_OUT * sum(sizes),
            bytes_accessed=sum(sizes) * D_OUT * 2,
            transcendentals=0,
        ),
        name="product_part",
    )(*operands)


def store_kernel(*refs):
    *pieces, out_hbm, zeros_ref, sems = refs

    def moved(sources):
        base = 0
        copies = []
        for place, source in enumerate(sources):
            width = source.shape[1]
            copies.append(
                pltpu.make_async_copy(source, out_hbm.at[:, pl.ds(base, width)], sems.at[place])
            )
            base += width
        for copy in copies:
            copy.start()
        for copy in copies:
            copy.wait()

    last = lax.axis_index("section") == SECTIONS - 1

    @pl.when(last)
    def _():
        zeros_ref[...] = jnp.zeros_like(zeros_ref)
        moved([zeros_ref] * (D_IN // CHUNK))

    @pl.when(jnp.logical_not(last))
    def _():
        moved(pieces)


def stored(pieces):
    return pl.pallas_call(
        store_kernel,
        out_shape=jax.ShapeDtypeStruct((TOKENS, D_IN), BF16),
        in_specs=[whole()] * len(pieces),
        out_specs=anywhere(),
        scratch_shapes=[
            VMEM((TOKENS, CHUNK), BF16),
            pltpu.SemaphoreType.DMA((D_IN // CHUNK,)),
        ],
        compiler_params=pltpu.CompilerParams(vmem_limit_bytes=8 * 2**20),
        cost_estimate=pl.CostEstimate(
            flops=0, bytes_accessed=4 * TOKENS * D_IN, transcendentals=0
        ),
        name="store",
    )(*[in_vmem(piece) for piece in pieces])


def replica(y, x, z):
    return (y % 4) * 8 + (x % 2) * 4 + z % 4


def moves(dy, dx, dz):
    return [
        (replica(y, x, z), replica(y + dy, x + dx, z + dz))
        for y in range(4)
        for x in range(2)
        for z in range(4)
    ]


def swaps(axis, masks):
    patterns = []
    for mask in masks:
        flip = [0, 0, 0]
        flip[axis] = mask
        patterns.append(
            [
                (replica(y, x, z), replica(y ^ flip[0], x ^ flip[1], z ^ flip[2]))
                for y in range(4)
                for x in range(2)
                for z in range(4)
            ]
        )
    return patterns


def ring(axis, steps):
    patterns = []
    for step in steps:
        shift = [0, 0, 0]
        shift[axis] = step
        patterns.append(moves(*shift))
    return patterns


X_ROUND = ring(1, (1,))
LEFT_Y_ROUND = swaps(0, (1, 3, 2))
LEFT_Z_ROUND = swaps(2, (1, 3, 2))
RIGHT_Z_ROUND = swaps(2, (1, 3, 2))
RIGHT_Y_ROUND = swaps(0, (1, 3, 2))


def sent(value, pattern):
    return [lax.ppermute(value, "dp", pairs) for pairs in pattern]


def tied(*values):
    return lax.optimization_barrier(values)


def handed(piece):
    return lax.ppermute(piece, "section", [(1, 0), (2, 1), (3, 2), (0, 3)])


def per_device(section_inputs, weights, output_grads, warm_start):
    weight = weights[0]
    value, grads, inputs, held = first_products(
        warm_start[0], output_grads[0], section_inputs[0], weight
    )

    arrivals = sent(value, X_ROUND)
    piece, held = product_part(grads, held, weight, 0)
    first = handed(piece)
    value = value + arrivals[0]

    value, held = tied(value, held)
    arrivals = sent(value, LEFT_Y_ROUND)
    piece, held = product_part(grads, held, weight, 1)
    second = handed(piece)
    value = (value + arrivals[0]) + (arrivals[1] + arrivals[2])

    value, held = tied(value, held)
    arrivals = sent(value, LEFT_Z_ROUND)
    (piece,) = product_part(grads, held, weight, 2)
    third = handed(piece)
    *pieces, first, _ = tied(value, *arrivals, first, piece)
    left, value = second_products(pieces, grads, inputs)

    arrivals = sent(value, RIGHT_Z_ROUND)
    tied_left, _ = tied(left, value)
    left_factor = left_stored(tied_left)
    value = widened(value, *arrivals).astype(WIRE)
    value, left_factor, second = tied(value, left_factor, second)
    arrivals = sent(value, RIGHT_Y_ROUND)
    value = widened(value, *arrivals)
    value, first, second, third = tied(value, first, second, third)
    value = value.astype(WIRE)
    arrivals = sent(value, X_ROUND)
    arrived = stored([first, second, third])
    right_factor = widened(value, *arrivals)
    return (arrived[None], left_factor[None], right_factor[None])


def solution(mesh):
    return jax.shard_map(
        per_device,
        mesh=mesh,
        in_specs=(
            P("section", "dp", None),
            P("section", None, None),
            P("section", "dp", None),
            P("section", None, None),
        ),
        out_specs=(P("section", "dp", None), P("section", None, None), P("section", None, None)),
        check_vma=False,
    )
```

time: 58.4 us -> 54.7 us (0.937)
  waiting for transfers between devices: 15.6 us -> 13.7 us
  Pallas kernels: 18.1 us -> 16.8 us
  starting transfers between devices: 23.7 us -> 22.6 us
  other arithmetic: 0.08 us -> 0.75 us
    ppermute x14, waiting for transfers between devices: 15.6 us -> 13.7 us  [sent(): return [lax.ppermute(value, 'dp', pairs) for pairs in pattern]]
    pallas_call x3 -> x2, Pallas kernels: 5.8 us -> 4.08 us  [the longest x1 3.43 us: first_products(): pl.pallas_call(first_kernel, out_shape=out_shape, in_specs=[anywhere()] *...]
    ppermute x14, starting transfers between devices: 23.5 us -> 22.3 us  [sent(): return [lax.ppermute(value, 'dp', pairs) for pairs in pattern]]
    broadcast_in_dim x0 -> x1, other arithmetic: none -> 0.65 us  [per_device(): return (arrived[None], left_factor[None], right_factor[None])]
  transfers between devices with their start and end apart: 17 -> 17, of which waited for: 9 -> 8; matrix products, arithmetic and copies ran while one was open for 0% -> 0% of each run, Pallas kernels for 24% -> 24%
where the time goes in v2:
time: 54.7 us; the launch traced here: 54.5 us
  starting transfers between devices  22.6 us (41%)
  Pallas kernels  16.8 us (31%)
  waiting for transfers between devices  13.7 us (25%)
  between operations  0.76 us (1%)
  other arithmetic  0.75 us (1%)
    ppermute x14, starting transfers between devices, sent(): return [lax.ppermute(value, 'dp', pairs) for pairs in pattern]  22.3 us
    ppermute x14, waiting for transfers between devices, sent(): return [lax.ppermute(value, 'dp', pairs) for pairs in pattern]  13.7 us
    pallas_call x3, Pallas kernels, product_part(): pl.pallas_call(functools.partial(product_kernel, base, sizes, ahead), out...  9.34 us
    pallas_call x1, Pallas kernels, first_products(): pl.pallas_call(first_kernel, out_shape=out_shape, in_specs=[anywhere()] *...  3.43 us
    pallas_call x1, Pallas kernels, second_products(): pl.pallas_call(second_kernel, out_shape=(VMEM((RANK, D_IN), F32), VMEM((R...  1.91 us
    pallas_call x1, Pallas kernels, stored(): pl.pallas_call(store_kernel, out_shape=jax.ShapeDtypeStruct((TOKENS, D_IN...  1.45 us
  transfers between devices with their start and end apart: 17, of which 8 were waited for; matrix products, arithmetic and copies ran while one was open for 0% of the time, Pallas kernels for 24%

profile of v2, /device:TPU:0, one launch (start us, length us, event | category | flops | bytes accessed | tf_op | source)
XLA Modules:
  0.0 54.5 jit_solution(481101344026409707)
XLA Ops:
  0.6 3.4 %first_products.1 = (f32[8,3072]{1,0:T(8,128)S(1)}, bf16[384,3072]{1,0:T(8,128)(2,1)S(1)}, bf16[384,3072]{1,0:T(8,128)(2,1)S(1)}, bf16[512,3072]{1,0:T(8,128)(2,1)S(1)}) custom-call(bf16[8,3072]{1,0:T(8,128)(2,1)} %bitcast.16, bf16[384,3072]{1,0:T(8,128)(2,1)} %bitcast.12, bf16[384,3072]{1,0:T(8,128)(2,1)} %bitcast.13, bf16[3072,3072]{1,0:T(8,128)(2,1)} %bitcast.8), custom_call_target="tpu_custom_call" | custom-call | flops 150994944 | bytes 4718592 | tf_op jit(solution)/shard_map/first_products/pallas_call | solution.py:123
  4.1 3.2 %collective-permute-start = (f32[8,3072]{1,0:T(8,128)S(1)}, f32[8,3072]{1,0:T(8,128)S(1)}, u32[]{:S(2)}, u32[]{:S(2)}) collective-permute-start(f32[8,3072]{1,0:T(8,128)S(1)} %get-tuple-element.30), channel_id=1, source_target_pairs={{0,16},{4,20},{8,24},{12,28},{16,0},{20,4},{24,8},{28,12},{32,48},... | collective-permute-start | bytes 294920 | tf_op jit(solution)/shard_map/ppermute | solution.py:380
  7.3 3.8 %product_part.3 = (bf16[384,1024]{1,0:T(8,128)(2,1)S(1)}, bf16[1024,3072]{1,0:T(8,128)(2,1)S(1)}) custom-call(bf16[384,3072]{1,0:T(8,128)(2,1)S(1)} %get-tuple-element.31.grads_ref, bf16[512,3072]{1,0:T(8,128)(2,1)S(1)} %get-tuple-element.32.refs_0_, bf16[3072,3072]{1,0:T(8,128)(2,1)} %bitcast.9), custom_call_target="tpu_custom_call" | custom-call | flops 2415919104 | bytes 6291456 | tf_op jit(solution)/shard_map/product_part/pallas_call | solution.py:271
  11.1 0.1 collective-permute-start.7
  11.1 0.0 collective-permute-done
  11.2 3.3 %collective-permute-start.3 = (f32[8,3072]{1,0:T(8,128)S(1)}, f32[8,3072]{1,0:T(8,128)S(1)}, u32[]{:S(2)}, u32[]{:S(2)}) collective-permute-start(f32[8,3072]{1,0:T(8,128)S(1)} %add.33), channel_id=1, source_target_pairs={{0,64},{4,68},{8,72},{12,76},{16,80},{20,84},{24,88},{28,92},{32,9... | collective-permute-start | bytes 294920 | tf_op jit(solution)/shard_map/ppermute | solution.py:380
  14.5 1.1 %collective-permute-start.2 = (f32[8,3072]{1,0:T(8,128)S(1)}, f32[8,3072]{1,0:T(8,128)S(1)}, u32[]{:S(2)}, u32[]{:S(2)}) collective-permute-start(f32[8,3072]{1,0:T(8,128)S(1)} %add.33), channel_id=1, source_target_pairs={{0,96},{4,100},{8,104},{12,108},{16,112},{20,116},{24,120},{28,124... | collective-permute-start | bytes 294920 | tf_op jit(solution)/shard_map/ppermute | solution.py:380
  15.5 0.0 collective-permute-start.1
  15.5 2.8 %product_part.4 = (bf16[384,1024]{1,0:T(8,128)(2,1)S(1)}, bf16[1024,3072]{1,0:T(8,128)(2,1)S(1)}) custom-call(bf16[384,3072]{1,0:T(8,128)(2,1)S(1)} %get-tuple-element.31.grads_ref, bf16[1024,3072]{1,0:T(8,128)(2,1)S(1)} %get-tuple-element.35.refs_0_, bf16[3072,3072]{1,0:T(8,128)(2,1)} %bitcast.10), custom_call_target="tpu_custom_call" | custom-call | flops 2415919104 | bytes 6291456 | tf_op jit(solution)/shard_map/product_part/pallas_call | solution.py:271
  18.4 0.2 collective-permute-start.11
  18.6 0.0 collective-permute-done.3
  18.6 2.0 %collective-permute-done.2 = f32[8,3072]{1,0:T(8,128)S(1)} collective-permute-done((f32[8,3072]{1,0:T(8,128)S(1)}, f32[8,3072]{1,0:T(8,128)S(1)}, u32[]{:S(2)}, u32[]{:S(2)}) %collective-permute-start.2) | collective-permute-done | bytes 98336 | tf_op jit(solution)/shard_map/ppermute | solution.py:380
  20.6 0.0 collective-permute-done.1
  20.6 4.0 %collective-permute-start.6 = (f32[8,3072]{1,0:T(8,128)S(1)}, f32[8,3072]{1,0:T(8,128)S(1)}, u32[]{:S(2)}, u32[]{:S(2)}) collective-permute-start(f32[8,3072]{1,0:T(8,128)S(1)} %add_add_fusion.own_ref), channel_id=1, source_target_pairs={{0,8},{4,12},{8,0},{12,4},{16,24},{20,28},{24,16},{28,20},{32,40},... | collective-permute-start | bytes 294920 | tf_op jit(solution)/shard_map/ppermute | solution.py:380
  24.6 0.7 %collective-permute-start.5 = (f32[8,3072]{1,0:T(8,128)S(1)}, f32[8,3072]{1,0:T(8,128)S(1)}, u32[]{:S(2)}, u32[]{:S(2)}) collective-permute-start(f32[8,3072]{1,0:T(8,128)S(1)} %add_add_fusion.own_ref), channel_id=1, source_target_pairs={{0,12},{4,8},{8,4},{12,0},{16,28},{20,24},{24,20},{28,16},{32,44},... | collective-permute-start | bytes 294920 | tf_op jit(solution)/shard_map/ppermute | solution.py:380
  25.3 0.3 collective-permute-start.4
  25.6 2.7 %product_part.5 = bf16[384,1024]{1,0:T(8,128)(2,1)S(1)} custom-call(bf16[384,3072]{1,0:T(8,128)(2,1)S(1)} %get-tuple-element.31.grads_ref, bf16[1024,3072]{1,0:T(8,128)(2,1)S(1)} %get-tuple-element.39.refs_0_, bf16[3072,3072]{1,0:T(8,128)(2,1)} %bitcast.11), custom_call_target="tpu_custom_call" | custom-call | flops 2415919104 | bytes 6291456 | tf_op jit(solution)/shard_map/product_part/pallas_call | solution.py:271
  28.3 0.0 collective-permute-done.6.c_ref
  28.3 2.1 %collective-permute-done.5.b_ref = f32[8,3072]{1,0:T(8,128)S(1)} collective-permute-done((f32[8,3072]{1,0:T(8,128)S(1)}, f32[8,3072]{1,0:T(8,128)S(1)}, u32[]{:S(2)}, u32[]{:S(2)}) %collective-permute-start.5) | collective-permute-done | bytes 98336 | tf_op jit(solution)/shard_map/ppermute | solution.py:380
  30.4 0.0 collective-permute-done.4.a_ref
  30.4 0.0 collective-permute-done.7.refs_0_
  30.4 1.9 %second_products.1 = (f32[8,3072]{1,0:T(8,128)S(1)}, bf16[8,3072]{1,0:T(8,128)(2,1)S(1)}) custom-call(f32[8,3072]{1,0:T(8,128)S(1)} %add_add_fusion.own_ref, f32[8,3072]{1,0:T(8,128)S(1)} %collective-permute-done.4.a_ref, f32[8,3072]{1,0:T(8,128)S(1)} %collective-permute-done.5.b_ref, f32[8,3072]{1,0:T(8,128)S(1)} %collective-permute-done.6.c_ref, ...), custom_call_target="tpu_custom_call" | custom-call | flops 150994944 | bytes 589824 | tf_op jit(solution)/shard_map/second_products/pallas_call | solution.py:182
  32.3 1.9 %collective-permute-start.10 = (bf16[8,3072]{1,0:T(8,128)(2,1)S(1)}, bf16[8,3072]{1,0:T(8,128)(2,1)S(1)}, u32[]{:S(2)}, u32[]{:S(2)}) collective-permute-start(bf16[8,3072]{1,0:T(8,128)(2,1)S(1)} %get-tuple-element.45), channel_id=1, source_target_pairs={{0,8},{4,12},{8,0},{12,4},{16,24},{20,28},{24,16},{28,20},{32,40},... | collective-permute-start | bytes 147464 | tf_op jit(solution)/shard_map/ppermute | solution.py:380
  34.3 1.2 %collective-permute-start.9 = (bf16[8,3072]{1,0:T(8,128)(2,1)S(1)}, bf16[8,3072]{1,0:T(8,128)(2,1)S(1)}, u32[]{:S(2)}, u32[]{:S(2)}) collective-permute-start(bf16[8,3072]{1,0:T(8,128)(2,1)S(1)} %get-tuple-element.45), channel_id=1, source_target_pairs={{0,12},{4,8},{8,4},{12,0},{16,28},{20,24},{24,20},{28,16},{32,44},... | collective-permute-start | bytes 147464 | tf_op jit(solution)/shard_map/ppermute | solution.py:380
  35.5 0.4 collective-permute-start.8
  35.9 0.0 collective-permute-start.15
  35.9 0.6 %left_stored.1 = f32[8,3072]{1,0:T(8,128)} custom-call(f32[8,3072]{1,0:T(8,128)S(1)} %get-tuple-element.46.left_ref), custom_call_target="tpu_custom_call" | custom-call | tf_op jit(solution)/shard_map/left_stored/pallas_call | solution.py:202
  36.5 1.9 %collective-permute-done.10 = bf16[8,3072]{1,0:T(8,128)(2,1)S(1)} collective-permute-done((bf16[8,3072]{1,0:T(8,128)(2,1)S(1)}, bf16[8,3072]{1,0:T(8,128)(2,1)S(1)}, u32[]{:S(2)}, u32[]{:S(2)}) %collective-permute-start.10) | collective-permute-done | bytes 49184 | tf_op jit(solution)/shard_map/ppermute | solution.py:380
  38.5 1.1 %collective-permute-done.9 = bf16[8,3072]{1,0:T(8,128)(2,1)S(1)} collective-permute-done((bf16[8,3072]{1,0:T(8,128)(2,1)S(1)}, bf16[8,3072]{1,0:T(8,128)(2,1)S(1)}, u32[]{:S(2)}, u32[]{:S(2)}) %collective-permute-start.9) | collective-permute-done | bytes 49184 | tf_op jit(solution)/shard_map/ppermute | solution.py:380
  39.6 0.0 collective-permute-done.8
  39.6 0.0 collective-permute-done.11.refs_1_
  39.6 2.7 %collective-permute-start.14 = (bf16[8,3072]{1,0:T(8,128)(2,1)S(1)}, bf16[8,3072]{1,0:T(8,128)(2,1)S(1)}, u32[]{:S(2)}, u32[]{:S(2)}) collective-permute-start(bf16[8,3072]{1,0:T(8,128)(2,1)S(1)} %add_convert_fusion), channel_id=1, source_target_pairs={{0,64},{4,68},{8,72},{12,76},{16,80},{20,84},{24,88},{28,92},{32,9... | collective-permute-start | bytes 147464 | tf_op jit(solution)/shard_map/ppermute | solution.py:380
  42.3 1.7 %collective-permute-start.13 = (bf16[8,3072]{1,0:T(8,128)(2,1)S(1)}, bf16[8,3072]{1,0:T(8,128)(2,1)S(1)}, u32[]{:S(2)}, u32[]{:S(2)}) collective-permute-start(bf16[8,3072]{1,0:T(8,128)(2,1)S(1)} %add_convert_fusion), channel_id=1, source_target_pairs={{0,96},{4,100},{8,104},{12,108},{16,112},{20,116},{24,120},{28,124... | collective-permute-start | bytes 147464 | tf_op jit(solution)/shard_map/ppermute | solution.py:380
  44.1 0.0 collective-permute-start.12
  44.1 1.4 %collective-permute-done.14 = bf16[8,3072]{1,0:T(8,128)(2,1)S(1)} collective-permute-done((bf16[8,3072]{1,0:T(8,128)(2,1)S(1)}, bf16[8,3072]{1,0:T(8,128)(2,1)S(1)}, u32[]{:S(2)}, u32[]{:S(2)}) %collective-permute-start.14) | collective-permute-done | bytes 49184 | tf_op jit(solution)/shard_map/ppermute | solution.py:380
  45.4 2.2 %collective-permute-done.13 = bf16[8,3072]{1,0:T(8,128)(2,1)S(1)} collective-permute-done((bf16[8,3072]{1,0:T(8,128)(2,1)S(1)}, bf16[8,3072]{1,0:T(8,128)(2,1)S(1)}, u32[]{:S(2)}, u32[]{:S(2)}) %collective-permute-start.13) | collective-permute-done | bytes 49184 | tf_op jit(solution)/shard_map/ppermute | solution.py:380
  47.6 0.5 collective-permute-done.12
  48.2 0.0 collective-permute-done.15.refs_2_
  48.2 1.8 %collective-permute-start.16 = (bf16[8,3072]{1,0:T(8,128)(2,1)S(1)}, bf16[8,3072]{1,0:T(8,128)(2,1)S(1)}, u32[]{:S(2)}, u32[]{:S(2)}) collective-permute-start(bf16[8,3072]{1,0:T(8,128)(2,1)S(1)} %convert_add_fusion), channel_id=1, source_target_pairs={{0,16},{4,20},{8,24},{12,28},{16,0},{20,4},{24,8},{28,12},{32,48},... | collective-permute-start | bytes 147464 | tf_op jit(solution)/shard_map/ppermute | solution.py:380
  50.0 1.4 %store.1 = bf16[384,3072]{1,0:T(8,128)(2,1)} custom-call(bf16[384,1024]{1,0:T(8,128)(2,1)S(1)} %collective-permute-done.7.refs_0_, bf16[384,1024]{1,0:T(8,128)(2,1)S(1)} %collective-permute-done.11.refs_1_, bf16[384,1024]{1,0:T(8,128)(2,1)S(1)} %collective-permute-done.15.refs_2_), custom_call_target="tpu_custom_call" | custom-call | bytes 4718592 | tf_op jit(solution)/shard_map/store/pallas_call | solution.py:317
  51.4 2.5 %collective-permute-done.16 = bf16[8,3072]{1,0:T(8,128)(2,1)S(1)} collective-permute-done((bf16[8,3072]{1,0:T(8,128)(2,1)S(1)}, bf16[8,3072]{1,0:T(8,128)(2,1)S(1)}, u32[]{:S(2)}, u32[]{:S(2)}) %collective-permute-start.16) | collective-permute-done | bytes 49184 | tf_op jit(solution)/shard_map/ppermute | solution.py:380
  53.9 0.7 %add_bitcast_fusion = f32[1,8,3072]{2,1,0:T(8,128)} fusion(bf16[8,3072]{1,0:T(8,128)(2,1)S(1)} %collective-permute-done.16, bf16[8,3072]{1,0:T(8,128)(2,1)S(1)} %convert_add_fusion), kind=kLoop, calls=%fused_computation | loop fusion | flops 73728 | bytes 196608 | tf_op jit(solution)/shard_map/broadcast_in_dim | solution.py:427
  (4 shorter events, 0.1 us)
Async XLA Ops:
  4.1 7.1 %collective-permute-start = (f32[8,3072]{1,0:T(8,128)S(1)}, f32[8,3072]{1,0:T(8,128)S(1)}, u32[]{:S(2)}, u32[]{:S(2)}) collective-permute-start(f32[8,3072]{1,0:T(8,128)S(1)} %get-tuple-element.30), channel_id=1, source_target_pairs={{0,16},{4,20},{8,24},{12,28},{16,0},{20,4},{24,8},{28,12},{32,48},... | collective-permute-start | bytes 294920 | tf_op jit(solution)/shard_map/ppermute | solution.py:380
  11.1 19.3 %collective-permute-start.7 = (bf16[384,1024]{1,0:T(8,128)(2,1)S(1)}, bf16[384,1024]{1,0:T(8,128)(2,1)S(1)}, u32[]{:S(2)}, u32[]{:S(2)}) collective-permute-start(bf16[384,1024]{1,0:T(8,128)(2,1)S(1)} %get-tuple-element.38), channel_id=1, source_target_pairs={{1,0},{2,1},{3,2},{0,3},{5,4},{6,5},{7,6},{4,7},{9,8},{10,9},{11,1... | collective-permute-start | bytes 2359304 | tf_op jit(solution)/shard_map/ppermute | solution.py:388
  11.2 7.4 %collective-permute-start.3 = (f32[8,3072]{1,0:T(8,128)S(1)}, f32[8,3072]{1,0:T(8,128)S(1)}, u32[]{:S(2)}, u32[]{:S(2)}) collective-permute-start(f32[8,3072]{1,0:T(8,128)S(1)} %add.33), channel_id=1, source_target_pairs={{0,64},{4,68},{8,72},{12,76},{16,80},{20,84},{24,88},{28,92},{32,9... | collective-permute-start | bytes 294920 | tf_op jit(solution)/shard_map/ppermute | solution.py:380
  14.5 6.1 %collective-permute-start.2 = (f32[8,3072]{1,0:T(8,128)S(1)}, f32[8,3072]{1,0:T(8,128)S(1)}, u32[]{:S(2)}, u32[]{:S(2)}) collective-permute-start(f32[8,3072]{1,0:T(8,128)S(1)} %add.33), channel_id=1, source_target_pairs={{0,96},{4,100},{8,104},{12,108},{16,112},{20,116},{24,120},{28,124... | collective-permute-start | bytes 294920 | tf_op jit(solution)/shard_map/ppermute | solution.py:380
  15.5 5.1 %collective-permute-start.1 = (f32[8,3072]{1,0:T(8,128)S(1)}, f32[8,3072]{1,0:T(8,128)S(1)}, u32[]{:S(2)}, u32[]{:S(2)}) collective-permute-start(f32[8,3072]{1,0:T(8,128)S(1)} %add.33), channel_id=1, source_target_pairs={{0,32},{4,36},{8,40},{12,44},{16,48},{20,52},{24,56},{28,60},{32,0... | collective-permute-start | bytes 294920 | tf_op jit(solution)/shard_map/ppermute | solution.py:380
  18.4 21.2 %collective-permute-start.11 = (bf16[384,1024]{1,0:T(8,128)(2,1)S(1)}, bf16[384,1024]{1,0:T(8,128)(2,1)S(1)}, u32[]{:S(2)}, u32[]{:S(2)}) collective-permute-start(bf16[384,1024]{1,0:T(8,128)(2,1)S(1)} %get-tuple-element.47), channel_id=1, source_target_pairs={{1,0},{2,1},{3,2},{0,3},{5,4},{6,5},{7,6},{4,7},{9,8},{10,9},{11,1... | collective-permute-start | bytes 2359304 | tf_op jit(solution)/shard_map/ppermute | solution.py:388
  20.6 7.7 %collective-permute-start.6 = (f32[8,3072]{1,0:T(8,128)S(1)}, f32[8,3072]{1,0:T(8,128)S(1)}, u32[]{:S(2)}, u32[]{:S(2)}) collective-permute-start(f32[8,3072]{1,0:T(8,128)S(1)} %add_add_fusion.own_ref), channel_id=1, source_target_pairs={{0,8},{4,12},{8,0},{12,4},{16,24},{20,28},{24,16},{28,20},{32,40},... | collective-permute-start | bytes 294920 | tf_op jit(solution)/shard_map/ppermute | solution.py:380
  24.6 5.8 %collective-permute-start.5 = (f32[8,3072]{1,0:T(8,128)S(1)}, f32[8,3072]{1,0:T(8,128)S(1)}, u32[]{:S(2)}, u32[]{:S(2)}) collective-permute-start(f32[8,3072]{1,0:T(8,128)S(1)} %add_add_fusion.own_ref), channel_id=1, source_target_pairs={{0,12},{4,8},{8,4},{12,0},{16,28},{20,24},{24,20},{28,16},{32,44},... | collective-permute-start | bytes 294920 | tf_op jit(solution)/shard_map/ppermute | solution.py:380
  25.3 5.1 %collective-permute-start.4 = (f32[8,3072]{1,0:T(8,128)S(1)}, f32[8,3072]{1,0:T(8,128)S(1)}, u32[]{:S(2)}, u32[]{:S(2)}) collective-permute-start(f32[8,3072]{1,0:T(8,128)S(1)} %add_add_fusion.own_ref), channel_id=1, source_target_pairs={{0,4},{4,0},{8,12},{12,8},{16,20},{20,16},{24,28},{28,24},{32,36},... | collective-permute-start | bytes 294920 | tf_op jit(solution)/shard_map/ppermute | solution.py:380
  32.3 6.2 %collective-permute-start.10 = (bf16[8,3072]{1,0:T(8,128)(2,1)S(1)}, bf16[8,3072]{1,0:T(8,128)(2,1)S(1)}, u32[]{:S(2)}, u32[]{:S(2)}) collective-permute-start(bf16[8,3072]{1,0:T(8,128)(2,1)S(1)} %get-tuple-element.45), channel_id=1, source_target_pairs={{0,8},{4,12},{8,0},{12,4},{16,24},{20,28},{24,16},{28,20},{32,40},... | collective-permute-start | bytes 147464 | tf_op jit(solution)/shard_map/ppermute | solution.py:380
  34.3 5.3 %collective-permute-start.9 = (bf16[8,3072]{1,0:T(8,128)(2,1)S(1)}, bf16[8,3072]{1,0:T(8,128)(2,1)S(1)}, u32[]{:S(2)}, u32[]{:S(2)}) collective-permute-start(bf16[8,3072]{1,0:T(8,128)(2,1)S(1)} %get-tuple-element.45), channel_id=1, source_target_pairs={{0,12},{4,8},{8,4},{12,0},{16,28},{20,24},{24,20},{28,16},{32,44},... | collective-permute-start | bytes 147464 | tf_op jit(solution)/shard_map/ppermute | solution.py:380
  35.5 4.1 %collective-permute-start.8 = (bf16[8,3072]{1,0:T(8,128)(2,1)S(1)}, bf16[8,3072]{1,0:T(8,128)(2,1)S(1)}, u32[]{:S(2)}, u32[]{:S(2)}) collective-permute-start(bf16[8,3072]{1,0:T(8,128)(2,1)S(1)} %get-tuple-element.45), channel_id=1, source_target_pairs={{0,4},{4,0},{8,12},{12,8},{16,20},{20,16},{24,28},{28,24},{32,36},... | collective-permute-start | bytes 147464 | tf_op jit(solution)/shard_map/ppermute | solution.py:380
  35.9 12.3 %collective-permute-start.15 = (bf16[384,1024]{1,0:T(8,128)(2,1)S(1)}, bf16[384,1024]{1,0:T(8,128)(2,1)S(1)}, u32[]{:S(2)}, u32[]{:S(2)}) collective-permute-start(bf16[384,1024]{1,0:T(8,128)(2,1)S(1)} %product_part.5), channel_id=1, source_target_pairs={{1,0},{2,1},{3,2},{0,3},{5,4},{6,5},{7,6},{4,7},{9,8},{10,9},{11,1... | collective-permute-start | bytes 2359304 | tf_op jit(solution)/shard_map/ppermute | solution.py:388
  39.6 5.8 %collective-permute-start.14 = (bf16[8,3072]{1,0:T(8,128)(2,1)S(1)}, bf16[8,3072]{1,0:T(8,128)(2,1)S(1)}, u32[]{:S(2)}, u32[]{:S(2)}) collective-permute-start(bf16[8,3072]{1,0:T(8,128)(2,1)S(1)} %add_convert_fusion), channel_id=1, source_target_pairs={{0,64},{4,68},{8,72},{12,76},{16,80},{20,84},{24,88},{28,92},{32,9... | collective-permute-start | bytes 147464 | tf_op jit(solution)/shard_map/ppermute | solution.py:380
  42.3 5.3 %collective-permute-start.13 = (bf16[8,3072]{1,0:T(8,128)(2,1)S(1)}, bf16[8,3072]{1,0:T(8,128)(2,1)S(1)}, u32[]{:S(2)}, u32[]{:S(2)}) collective-permute-start(bf16[8,3072]{1,0:T(8,128)(2,1)S(1)} %add_convert_fusion), channel_id=1, source_target_pairs={{0,96},{4,100},{8,104},{12,108},{16,112},{20,116},{24,120},{28,124... | collective-permute-start | bytes 147464 | tf_op jit(solution)/shard_map/ppermute | solution.py:380
  44.1 4.1 %collective-permute-start.12 = (bf16[8,3072]{1,0:T(8,128)(2,1)S(1)}, bf16[8,3072]{1,0:T(8,128)(2,1)S(1)}, u32[]{:S(2)}, u32[]{:S(2)}) collective-permute-start(bf16[8,3072]{1,0:T(8,128)(2,1)S(1)} %add_convert_fusion), channel_id=1, source_target_pairs={{0,32},{4,36},{8,40},{12,44},{16,48},{20,52},{24,56},{28,60},{32,0... | collective-permute-start | bytes 147464 | tf_op jit(solution)/shard_map/ppermute | solution.py:380
  48.2 5.7 %collective-permute-start.16 = (bf16[8,3072]{1,0:T(8,128)(2,1)S(1)}, bf16[8,3072]{1,0:T(8,128)(2,1)S(1)}, u32[]{:S(2)}, u32[]{:S(2)}) collective-permute-start(bf16[8,3072]{1,0:T(8,128)(2,1)S(1)} %convert_add_fusion), channel_id=1, source_target_pairs={{0,16},{4,20},{8,24},{12,28},{16,0},{20,4},{24,8},{28,12},{32,48},... | collective-permute-start | bytes 147464 | tf_op jit(solution)/shard_map/ppermute | solution.py:380

commit v3 on v2

--- a/solution.py
+++ b/solution.py
@@ -13,10 +13,10 @@
 RANK = 8
 REPLICAS = 32
 SECTIONS = 4
-ROW_PARTS = 3
-WINDOW = 4
+ROW_PARTS = (128, 128, 128)
 WIRE = jnp.bfloat16
 CHUNK = 512
+SHARE = 4
 PARTS = ((512, 512), (1024, 0), (1024, 0))
 
 VMEM = pltpu.VMEM
@@ -62,12 +62,13 @@
     if ahead:
         ahead_ref, refs = refs[0], refs[1:]
     warm_ref, sems = refs
-    rows = TOKENS // ROW_PARTS
     warm_copy = pltpu.make_async_copy(warm_hbm, warm_ref, sems.at[0])
     warm_copy.start()
+    spans = []
     copies = []
-    for part in range(ROW_PARTS):
-        span = pl.ds(part * rows, rows)
+    first = 0
+    for part, rows in enumerate(ROW_PARTS):
+        span = pl.ds(first, rows)
         copies.append(
             (
                 pltpu.make_async_copy(
@@ -78,30 +79,24 @@
                 ),
             )
         )
+        spans.append(slice(first, first + rows))
+        first += rows
+    for pair in copies:
+        for copy in pair:
+            copy.start()
     if ahead:
         ahead_copy = pltpu.make_async_copy(
             weight_hbm.at[pl.ds(0, ahead)], ahead_ref, sems.at[1]
         )
-
-    def start(part):
-        if part < ROW_PARTS:
-            for copy in copies[part]:
-                copy.start()
-        elif ahead and part == ROW_PARTS:
-            ahead_copy.start()
-
-    for part in range(WINDOW):
-        start(part)
+        ahead_copy.start()
     warm_copy.wait()
     total = None
-    for part in range(ROW_PARTS):
-        span = slice(part * rows, (part + 1) * rows)
-        copies[part][0].wait()
-        start(part + WINDOW)
+    for span, (grads_copy, inputs_copy) in zip(spans, copies):
+        grads_copy.wait()
         projected = stacked(
             lax.dot_general(warm_ref[...], grads_ref[span, :], NT, preferred_element_type=F32)
         )
-        copies[part][1].wait()
+        inputs_copy.wait()
         term = lax.dot_general(
             projected, inputs_ref[span, :], NN, preferred_element_type=F32
         )
@@ -127,7 +122,7 @@
         out_specs=[whole()] * len(out_shape),
         scratch_shapes=[
             VMEM((RANK, D_OUT), BF16),
-            pltpu.SemaphoreType.DMA((2 + 2 * ROW_PARTS,)),
+            pltpu.SemaphoreType.DMA((2 + 2 * len(ROW_PARTS),)),
         ],
         compiler_params=pltpu.CompilerParams(vmem_limit_bytes=16 * 2**20),
         cost_estimate=pl.CostEstimate(
@@ -162,8 +157,9 @@
     return result
 
 
-def second_kernel(own_ref, a_ref, b_ref, c_ref, grads_ref, inputs_ref, left_ref, partial_ref):
-    total = (own_ref[...] + a_ref[...]) + (b_ref[...] + c_ref[...])
+def second_kernel(*refs):
+    *piece_refs, grads_ref, inputs_ref, left_ref, partial_ref = refs
+    total = functools.reduce(lambda left, right: left + right, [ref[...] for ref in piece_refs])
     total = total * (1.0 / REPLICAS)
     left_ref[...] = total
     steps = gram_schmidt_steps(total)
@@ -182,7 +178,7 @@
     return pl.pallas_call(
         second_kernel,
         out_shape=(VMEM((RANK, D_IN), F32), VMEM((RANK, D_OUT), WIRE)),
-        in_specs=[whole()] * 6,
+        in_specs=[whole()] * (len(pieces) + 2),
         out_specs=(whole(), whole()),
         compiler_params=pltpu.CompilerParams(vmem_limit_bytes=16 * 2**20),
         cost_estimate=pl.CostEstimate(
@@ -276,8 +272,8 @@
         scratch_shapes=scratch,
         compiler_params=pltpu.CompilerParams(vmem_limit_bytes=32 * 2**20),
         cost_estimate=pl.CostEstimate(
-            flops=2 * TOKENS * D_OUT * sum(sizes),
-            bytes_accessed=sum(sizes) * D_OUT * 2,
+            flops=2 * TOKENS * D_OUT * sum(sizes) // SHARE,
+            bytes_accessed=sum(sizes) * D_OUT * 2 // SHARE,
             transcendentals=0,
         ),
         name="product_part",
@@ -344,36 +340,24 @@
     ]
 
 
-def swaps(axis, masks):
-    patterns = []
-    for mask in masks:
-        flip = [0, 0, 0]
-        flip[axis] = mask
-        patterns.append(
-            [
-                (replica(y, x, z), replica(y ^ flip[0], x ^ flip[1], z ^ flip[2]))
-                for y in range(4)
-                for x in range(2)
-                for z in range(4)
-            ]
-        )
-    return patterns
-
-
-def ring(axis, steps):
-    patterns = []
-    for step in steps:
-        shift = [0, 0, 0]
-        shift[axis] = step
-        patterns.append(moves(*shift))
-    return patterns
-
-
-X_ROUND = ring(1, (1,))
-LEFT_Y_ROUND = swaps(0, (1, 3, 2))
-LEFT_Z_ROUND = swaps(2, (1, 3, 2))
-RIGHT_Z_ROUND = swaps(2, (1, 3, 2))
-RIGHT_Y_ROUND = swaps(0, (1, 3, 2))
+def swaps(*masks):
+    return [
+        [
+            (replica(y, x, z), replica(y ^ flip_y, x ^ flip_x, z ^ flip_z))
+            for y in range(4)
+            for x in range(2)
+            for z in range(4)
+        ]
+        for flip_y, flip_x, flip_z in masks
+    ]
+
+
+X_ROUND = swaps((0, 1, 0))
+Y_ROUND = swaps((1, 0, 0), (3, 0, 0), (2, 0, 0))
+Z_ROUND = swaps((0, 0, 1), (0, 0, 3), (0, 0, 2))
+LEFT_ROUNDS = [X_ROUND, Z_ROUND, Y_ROUND]
+PART_OF_ROUND = {0: 0, 1: 1, 2: 2}
+RIGHT_ROUNDS = [Z_ROUND, Y_ROUND, X_ROUND]
 
 
 def sent(value, pattern):
@@ -394,35 +378,32 @@
         warm_start[0], output_grads[0], section_inputs[0], weight
     )
 
-    arrivals = sent(value, X_ROUND)
-    piece, held = product_part(grads, held, weight, 0)
-    first = handed(piece)
-    value = value + arrivals[0]
-
-    value, held = tied(value, held)
-    arrivals = sent(value, LEFT_Y_ROUND)
-    piece, held = product_part(grads, held, weight, 1)
-    second = handed(piece)
-    value = (value + arrivals[0]) + (arrivals[1] + arrivals[2])
-
-    value, held = tied(value, held)
-    arrivals = sent(value, LEFT_Z_ROUND)
-    (piece,) = product_part(grads, held, weight, 2)
-    third = handed(piece)
-    *pieces, first, _ = tied(value, *arrivals, first, piece)
+    arrived = []
+    for place, pattern in enumerate(LEFT_ROUNDS):
+        if place:
+            value = widened(value, *arrivals)
+            value, held = tied(value, held)
+        arrivals = sent(value, pattern)
+        part = PART_OF_ROUND.get(place)
+        if part is not None:
+            piece, *held = product_part(grads, held, weight, part)
+            held = held[0] if held else piece
+            arrived.append(handed(piece))
+    *pieces, arrived[0], _ = tied(value, *arrivals, arrived[0], held)
     left, value = second_products(pieces, grads, inputs)
 
-    arrivals = sent(value, RIGHT_Z_ROUND)
-    tied_left, _ = tied(left, value)
-    left_factor = left_stored(tied_left)
-    value = widened(value, *arrivals).astype(WIRE)
-    value, left_factor, second = tied(value, left_factor, second)
-    arrivals = sent(value, RIGHT_Y_ROUND)
-    value = widened(value, *arrivals)
-    value, first, second, third = tied(value, first, second, third)
-    value = value.astype(WIRE)
-    arrivals = sent(value, X_ROUND)
-    arrived = stored([first, second, third])
+    for place, pattern in enumerate(RIGHT_ROUNDS):
+        if place:
+            value = widened(value, *arrivals).astype(WIRE)
+        if place == len(RIGHT_ROUNDS) - 1:
+            value, *arrived = tied(value, *arrived)
+        elif place == 1:
+            value, left_factor, *arrived[:-1] = tied(value, left_factor, *arrived[:-1])
+        arrivals = sent(value, pattern)
+        if not place:
+            tied_left, _ = tied(left, value)
+            left_factor = left_stored(tied_left)
+    arrived = stored(arrived)
     right_factor = widened(value, *arrivals)
     return (arrived[None], left_factor[None], right_factor[None])
 

time: 54.7 us -> 54 us (0.987)
  transfers between devices with their start and end apart: 17 -> 17, of which waited for: 8 -> 8; matrix products, arithmetic and copies ran while one was open for 0% -> 0% of each run, Pallas kernels for 24% -> 25%
where the time goes in v3:
time: 54 us; the launch traced here: 53.9 us
  starting transfers between devices  22.4 us (41%)
  Pallas kernels  16.8 us (31%)
  waiting for transfers between devices  13.2 us (24%)
  between operations  0.76 us (1%)
  other arithmetic  0.74 us (1%)
    ppermute x14, starting transfers between devices, sent(): return [lax.ppermute(value, 'dp', pairs) for pairs in pattern]  22.4 us
    ppermute x14, waiting for transfers between devices, sent(): return [lax.ppermute(value, 'dp', pairs) for pairs in pattern]  13.2 us
    pallas_call x3, Pallas kernels, product_part(): pl.pallas_call(functools.partial(product_kernel, base, sizes, ahead), out...  9.35 us
    pallas_call x1, Pallas kernels, first_products(): pl.pallas_call(first_kernel, out_shape=out_shape, in_specs=[anywhere()] *...  3.43 us
    pallas_call x1, Pallas kernels, second_products(): pl.pallas_call(second_kernel, out_shape=(VMEM((RANK, D_IN), F32), VMEM((R...  1.91 us
    pallas_call x1, Pallas kernels, stored(): pl.pallas_call(store_kernel, out_shape=jax.ShapeDtypeStruct((TOKENS, D_IN...  1.45 us
  transfers between devices with their start and end apart: 17, of which 8 were waited for; matrix products, arithmetic and copies ran while one was open for 0% of the time, Pallas kernels for 25%

profile of v3, /device:TPU:0, one launch (start us, length us, event | category | flops | bytes accessed | tf_op | source)
XLA Modules:
  0.0 53.9 jit_solution(16464036330854529591)
XLA Ops:
  0.6 3.4 %first_products.1 = (f32[8,3072]{1,0:T(8,128)S(1)}, bf16[384,3072]{1,0:T(8,128)(2,1)S(1)}, bf16[384,3072]{1,0:T(8,128)(2,1)S(1)}, bf16[512,3072]{1,0:T(8,128)(2,1)S(1)}) custom-call(bf16[8,3072]{1,0:T(8,128)(2,1)} %bitcast.16, bf16[384,3072]{1,0:T(8,128)(2,1)} %bitcast.12, bf16[384,3072]{1,0:T(8,128)(2,1)} %bitcast.13, bf16[3072,3072]{1,0:T(8,128)(2,1)} %bitcast.8), custom_call_target="tpu_custom_call" | custom-call | flops 150994944 | bytes 4718592 | tf_op jit(solution)/shard_map/first_products/pallas_call | solution.py:118
  4.1 3.2 %collective-permute-start = (f32[8,3072]{1,0:T(8,128)S(1)}, f32[8,3072]{1,0:T(8,128)S(1)}, u32[]{:S(2)}, u32[]{:S(2)}) collective-permute-start(f32[8,3072]{1,0:T(8,128)S(1)} %get-tuple-element.31), channel_id=1, source_target_pairs={{0,16},{4,20},{8,24},{12,28},{16,0},{20,4},{24,8},{28,12},{32,48},... | collective-permute-start | bytes 294920 | tf_op jit(solution)/shard_map/ppermute | solution.py:364
  7.3 3.8 %product_part.3 = (bf16[384,1024]{1,0:T(8,128)(2,1)S(1)}, bf16[1024,3072]{1,0:T(8,128)(2,1)S(1)}) custom-call(bf16[384,3072]{1,0:T(8,128)(2,1)S(1)} %get-tuple-element.32.grads_ref.refs_4_, bf16[512,3072]{1,0:T(8,128)(2,1)S(1)} %get-tuple-element.33.refs_0_, bf16[3072,3072]{1,0:T(8,128)(2,1)} %bitcast.9), custom_call_target="tpu_custom_call" | custom-call | flops 603979776 | bytes 1572864 | tf_op jit(solution)/shard_map/product_part/pallas_call | solution.py:267
  11.1 0.0 collective-permute-done
  11.1 4.0 %collective-permute-start.3 = (f32[8,3072]{1,0:T(8,128)S(1)}, f32[8,3072]{1,0:T(8,128)S(1)}, u32[]{:S(2)}, u32[]{:S(2)}) collective-permute-start(f32[8,3072]{1,0:T(8,128)S(1)} %add.33), channel_id=1, source_target_pairs={{0,8},{4,12},{8,0},{12,4},{16,24},{20,28},{24,16},{28,20},{32,40},... | collective-permute-start | bytes 294920 | tf_op jit(solution)/shard_map/ppermute | solution.py:364
  15.1 0.7 %collective-permute-start.2 = (f32[8,3072]{1,0:T(8,128)S(1)}, f32[8,3072]{1,0:T(8,128)S(1)}, u32[]{:S(2)}, u32[]{:S(2)}) collective-permute-start(f32[8,3072]{1,0:T(8,128)S(1)} %add.33), channel_id=1, source_target_pairs={{0,12},{4,8},{8,4},{12,0},{16,28},{20,24},{24,20},{28,16},{32,44},... | collective-permute-start | bytes 294920 | tf_op jit(solution)/shard_map/ppermute | solution.py:364
  15.8 0.3 collective-permute-start.1
  16.1 0.0 collective-permute-start.7
  16.1 2.8 %product_part.4 = (bf16[384,1024]{1,0:T(8,128)(2,1)S(1)}, bf16[1024,3072]{1,0:T(8,128)(2,1)S(1)}) custom-call(bf16[384,3072]{1,0:T(8,128)(2,1)S(1)} %get-tuple-element.32.grads_ref.refs_4_, bf16[1024,3072]{1,0:T(8,128)(2,1)S(1)} %get-tuple-element.36.refs_0_, bf16[3072,3072]{1,0:T(8,128)(2,1)} %bitcast.10), custom_call_target="tpu_custom_call" | custom-call | flops 603979776 | bytes 1572864 | tf_op jit(solution)/shard_map/product_part/pallas_call | solution.py:267
  18.9 0.0 collective-permute-done.3
  18.9 1.9 %collective-permute-done.2 = f32[8,3072]{1,0:T(8,128)S(1)} collective-permute-done((f32[8,3072]{1,0:T(8,128)S(1)}, f32[8,3072]{1,0:T(8,128)S(1)}, u32[]{:S(2)}, u32[]{:S(2)}) %collective-permute-start.2) | collective-permute-done | bytes 98336 | tf_op jit(solution)/shard_map/ppermute | solution.py:364
  20.9 0.0 collective-permute-done.1
  20.9 3.3 %collective-permute-start.6 = (f32[8,3072]{1,0:T(8,128)S(1)}, f32[8,3072]{1,0:T(8,128)S(1)}, u32[]{:S(2)}, u32[]{:S(2)}) collective-permute-start(f32[8,3072]{1,0:T(8,128)S(1)} %add_add_fusion.refs_0_), channel_id=1, source_target_pairs={{0,64},{4,68},{8,72},{12,76},{16,80},{20,84},{24,88},{28,92},{32,9... | collective-permute-start | bytes 294920 | tf_op jit(solution)/shard_map/ppermute | solution.py:364
  24.2 1.1 %collective-permute-start.5 = (f32[8,3072]{1,0:T(8,128)S(1)}, f32[8,3072]{1,0:T(8,128)S(1)}, u32[]{:S(2)}, u32[]{:S(2)}) collective-permute-start(f32[8,3072]{1,0:T(8,128)S(1)} %add_add_fusion.refs_0_), channel_id=1, source_target_pairs={{0,96},{4,100},{8,104},{12,108},{16,112},{20,116},{24,120},{28,124... | collective-permute-start | bytes 294920 | tf_op jit(solution)/shard_map/ppermute | solution.py:364
  25.2 0.0 collective-permute-start.4
  25.2 0.0 collective-permute-start.11
  25.2 2.7 %product_part.5 = bf16[384,1024]{1,0:T(8,128)(2,1)S(1)} custom-call(bf16[384,3072]{1,0:T(8,128)(2,1)S(1)} %get-tuple-element.32.grads_ref.refs_4_, bf16[1024,3072]{1,0:T(8,128)(2,1)S(1)} %get-tuple-element.40.refs_0_, bf16[3072,3072]{1,0:T(8,128)(2,1)} %bitcast.11), custom_call_target="tpu_custom_call" | custom-call | flops 603979776 | bytes 1572864 | tf_op jit(solution)/shard_map/product_part/pallas_call | solution.py:267
  27.9 0.0 collective-permute-done.6.refs_3_
  28.0 2.1 %collective-permute-done.5.refs_2_ = f32[8,3072]{1,0:T(8,128)S(1)} collective-permute-done((f32[8,3072]{1,0:T(8,128)S(1)}, f32[8,3072]{1,0:T(8,128)S(1)}, u32[]{:S(2)}, u32[]{:S(2)}) %collective-permute-start.5) | collective-permute-done | bytes 98336 | tf_op jit(solution)/shard_map/ppermute | solution.py:364
  30.0 0.0 collective-permute-done.4.refs_1_
  30.0 0.0 collective-permute-done.7.refs_0_
  30.0 1.9 %second_products.1 = (f32[8,3072]{1,0:T(8,128)S(1)}, bf16[8,3072]{1,0:T(8,128)(2,1)S(1)}) custom-call(f32[8,3072]{1,0:T(8,128)S(1)} %add_add_fusion.refs_0_, f32[8,3072]{1,0:T(8,128)S(1)} %collective-permute-done.4.refs_1_, f32[8,3072]{1,0:T(8,128)S(1)} %collective-permute-done.5.refs_2_, f32[8,3072]{1,0:T(8,128)S(1)} %collective-permute-done.6.refs_3_, ...), custom_call_target="tpu_custom_call" | custom-call | flops 150994944 | bytes 589824 | tf_op jit(solution)/shard_map/second_products/pallas_call | solution.py:178
  31.9 2.2 %collective-permute-start.10 = (bf16[8,3072]{1,0:T(8,128)(2,1)S(1)}, bf16[8,3072]{1,0:T(8,128)(2,1)S(1)}, u32[]{:S(2)}, u32[]{:S(2)}) collective-permute-start(bf16[8,3072]{1,0:T(8,128)(2,1)S(1)} %get-tuple-element.46), channel_id=1, source_target_pairs={{0,8},{4,12},{8,0},{12,4},{16,24},{20,28},{24,16},{28,20},{32,40},... | collective-permute-start | bytes 147464 | tf_op jit(solution)/shard_map/ppermute | solution.py:364
  34.1 1.1 %collective-permute-start.9 = (bf16[8,3072]{1,0:T(8,128)(2,1)S(1)}, bf16[8,3072]{1,0:T(8,128)(2,1)S(1)}, u32[]{:S(2)}, u32[]{:S(2)}) collective-permute-start(bf16[8,3072]{1,0:T(8,128)(2,1)S(1)} %get-tuple-element.46), channel_id=1, source_target_pairs={{0,12},{4,8},{8,4},{12,0},{16,28},{20,24},{24,20},{28,16},{32,44},... | collective-permute-start | bytes 147464 | tf_op jit(solution)/shard_map/ppermute | solution.py:364
  35.3 0.2 collective-permute-start.8
  35.5 0.0 collective-permute-start.15
  35.5 0.6 %left_stored.1 = f32[8,3072]{1,0:T(8,128)} custom-call(f32[8,3072]{1,0:T(8,128)S(1)} %get-tuple-element.47.left_ref), custom_call_target="tpu_custom_call" | custom-call | tf_op jit(solution)/shard_map/left_stored/pallas_call | solution.py:198
  36.2 1.6 %collective-permute-done.10 = bf16[8,3072]{1,0:T(8,128)(2,1)S(1)} collective-permute-done((bf16[8,3072]{1,0:T(8,128)(2,1)S(1)}, bf16[8,3072]{1,0:T(8,128)(2,1)S(1)}, u32[]{:S(2)}, u32[]{:S(2)}) %collective-permute-start.10) | collective-permute-done | bytes 49184 | tf_op jit(solution)/shard_map/ppermute | solution.py:364
  37.7 1.7 %collective-permute-done.9 = bf16[8,3072]{1,0:T(8,128)(2,1)S(1)} collective-permute-done((bf16[8,3072]{1,0:T(8,128)(2,1)S(1)}, bf16[8,3072]{1,0:T(8,128)(2,1)S(1)}, u32[]{:S(2)}, u32[]{:S(2)}) %collective-permute-start.9) | collective-permute-done | bytes 49184 | tf_op jit(solution)/shard_map/ppermute | solution.py:364
  39.4 0.0 collective-permute-done.8
  39.5 0.0 collective-permute-done.11.refs_1_
  39.5 2.0 %collective-permute-start.14 = (bf16[8,3072]{1,0:T(8,128)(2,1)S(1)}, bf16[8,3072]{1,0:T(8,128)(2,1)S(1)}, u32[]{:S(2)}, u32[]{:S(2)}) collective-permute-start(bf16[8,3072]{1,0:T(8,128)(2,1)S(1)} %add_convert_fusion.1), channel_id=1, source_target_pairs={{0,64},{4,68},{8,72},{12,76},{16,80},{20,84},{24,88},{28,92},{32,9... | collective-permute-start | bytes 147464 | tf_op jit(solution)/shard_map/ppermute | solution.py:364
  41.4 2.0 %collective-permute-start.13 = (bf16[8,3072]{1,0:T(8,128)(2,1)S(1)}, bf16[8,3072]{1,0:T(8,128)(2,1)S(1)}, u32[]{:S(2)}, u32[]{:S(2)}) collective-permute-start(bf16[8,3072]{1,0:T(8,128)(2,1)S(1)} %add_convert_fusion.1), channel_id=1, source_target_pairs={{0,96},{4,100},{8,104},{12,108},{16,112},{20,116},{24,120},{28,124... | collective-permute-start | bytes 147464 | tf_op jit(solution)/shard_map/ppermute | solution.py:364
  43.4 0.0 collective-permute-start.12
  43.4 2.1 %collective-permute-done.14 = bf16[8,3072]{1,0:T(8,128)(2,1)S(1)} collective-permute-done((bf16[8,3072]{1,0:T(8,128)(2,1)S(1)}, bf16[8,3072]{1,0:T(8,128)(2,1)S(1)}, u32[]{:S(2)}, u32[]{:S(2)}) %collective-permute-start.14) | collective-permute-done | bytes 49184 | tf_op jit(solution)/shard_map/ppermute | solution.py:364
  45.6 1.2 %collective-permute-done.13 = bf16[8,3072]{1,0:T(8,128)(2,1)S(1)} collective-permute-done((bf16[8,3072]{1,0:T(8,128)(2,1)S(1)}, bf16[8,3072]{1,0:T(8,128)(2,1)S(1)}, u32[]{:S(2)}, u32[]{:S(2)}) %collective-permute-start.13) | collective-permute-done | bytes 49184 | tf_op jit(solution)/shard_map/ppermute | solution.py:364
  46.7 0.8 %collective-permute-done.12 = bf16[8,3072]{1,0:T(8,128)(2,1)S(1)} collective-permute-done((bf16[8,3072]{1,0:T(8,128)(2,1)S(1)}, bf16[8,3072]{1,0:T(8,128)(2,1)S(1)}, u32[]{:S(2)}, u32[]{:S(2)}) %collective-permute-start.12) | collective-permute-done | bytes 49184 | tf_op jit(solution)/shard_map/ppermute | solution.py:364
  47.6 0.0 collective-permute-done.15.refs_2_
  47.6 2.4 %collective-permute-start.16 = (bf16[8,3072]{1,0:T(8,128)(2,1)S(1)}, bf16[8,3072]{1,0:T(8,128)(2,1)S(1)}, u32[]{:S(2)}, u32[]{:S(2)}) collective-permute-start(bf16[8,3072]{1,0:T(8,128)(2,1)S(1)} %add_convert_fusion), channel_id=1, source_target_pairs={{0,16},{4,20},{8,24},{12,28},{16,0},{20,4},{24,8},{28,12},{32,48},... | collective-permute-start | bytes 147464 | tf_op jit(solution)/shard_map/ppermute | solution.py:364
  49.9 1.4 %store.1 = bf16[384,3072]{1,0:T(8,128)(2,1)} custom-call(bf16[384,1024]{1,0:T(8,128)(2,1)S(1)} %collective-permute-done.7.refs_0_, bf16[384,1024]{1,0:T(8,128)(2,1)S(1)} %collective-permute-done.11.refs_1_, bf16[384,1024]{1,0:T(8,128)(2,1)S(1)} %collective-permute-done.15.refs_2_), custom_call_target="tpu_custom_call" | custom-call | bytes 4718592 | tf_op jit(solution)/shard_map/store/pallas_call | solution.py:313
  51.4 1.8 %collective-permute-done.16 = bf16[8,3072]{1,0:T(8,128)(2,1)S(1)} collective-permute-done((bf16[8,3072]{1,0:T(8,128)(2,1)S(1)}, bf16[8,3072]{1,0:T(8,128)(2,1)S(1)}, u32[]{:S(2)}, u32[]{:S(2)}) %collective-permute-start.16) | collective-permute-done | bytes 49184 | tf_op jit(solution)/shard_map/ppermute | solution.py:364
  53.2 0.7 %add_bitcast_fusion = f32[1,8,3072]{2,1,0:T(8,128)} fusion(bf16[8,3072]{1,0:T(8,128)(2,1)S(1)} %collective-permute-done.16, bf16[8,3072]{1,0:T(8,128)(2,1)S(1)} %add_convert_fusion), kind=kLoop, calls=%fused_computation | loop fusion | flops 73728 | bytes 196608 | tf_op jit(solution)/shard_map/broadcast_in_dim | solution.py:408
  (4 shorter events, 0.1 us)
Async XLA Ops:
  4.1 7.0 %collective-permute-start = (f32[8,3072]{1,0:T(8,128)S(1)}, f32[8,3072]{1,0:T(8,128)S(1)}, u32[]{:S(2)}, u32[]{:S(2)}) collective-permute-start(f32[8,3072]{1,0:T(8,128)S(1)} %get-tuple-element.31), channel_id=1, source_target_pairs={{0,16},{4,20},{8,24},{12,28},{16,0},{20,4},{24,8},{28,12},{32,48},... | collective-permute-start | bytes 294920 | tf_op jit(solution)/shard_map/ppermute | solution.py:364
  11.1 7.8 %collective-permute-start.3 = (f32[8,3072]{1,0:T(8,128)S(1)}, f32[8,3072]{1,0:T(8,128)S(1)}, u32[]{:S(2)}, u32[]{:S(2)}) collective-permute-start(f32[8,3072]{1,0:T(8,128)S(1)} %add.33), channel_id=1, source_target_pairs={{0,8},{4,12},{8,0},{12,4},{16,24},{20,28},{24,16},{28,20},{32,40},... | collective-permute-start | bytes 294920 | tf_op jit(solution)/shard_map/ppermute | solution.py:364
  15.1 5.8 %collective-permute-start.2 = (f32[8,3072]{1,0:T(8,128)S(1)}, f32[8,3072]{1,0:T(8,128)S(1)}, u32[]{:S(2)}, u32[]{:S(2)}) collective-permute-start(f32[8,3072]{1,0:T(8,128)S(1)} %add.33), channel_id=1, source_target_pairs={{0,12},{4,8},{8,4},{12,0},{16,28},{20,24},{24,20},{28,16},{32,44},... | collective-permute-start | bytes 294920 | tf_op jit(solution)/shard_map/ppermute | solution.py:364
  15.8 5.1 %collective-permute-start.1 = (f32[8,3072]{1,0:T(8,128)S(1)}, f32[8,3072]{1,0:T(8,128)S(1)}, u32[]{:S(2)}, u32[]{:S(2)}) collective-permute-start(f32[8,3072]{1,0:T(8,128)S(1)} %add.33), channel_id=1, source_target_pairs={{0,4},{4,0},{8,12},{12,8},{16,20},{20,16},{24,28},{28,24},{32,36},... | collective-permute-start | bytes 294920 | tf_op jit(solution)/shard_map/ppermute | solution.py:364
  16.1 13.9 %collective-permute-start.7 = (bf16[384,1024]{1,0:T(8,128)(2,1)S(1)}, bf16[384,1024]{1,0:T(8,128)(2,1)S(1)}, u32[]{:S(2)}, u32[]{:S(2)}) collective-permute-start(bf16[384,1024]{1,0:T(8,128)(2,1)S(1)} %get-tuple-element.39), channel_id=1, source_target_pairs={{1,0},{2,1},{3,2},{0,3},{5,4},{6,5},{7,6},{4,7},{9,8},{10,9},{11,1... | collective-permute-start | bytes 2359304 | tf_op jit(solution)/shard_map/ppermute | solution.py:372
  20.9 7.0 %collective-permute-start.6 = (f32[8,3072]{1,0:T(8,128)S(1)}, f32[8,3072]{1,0:T(8,128)S(1)}, u32[]{:S(2)}, u32[]{:S(2)}) collective-permute-start(f32[8,3072]{1,0:T(8,128)S(1)} %add_add_fusion.refs_0_), channel_id=1, source_target_pairs={{0,64},{4,68},{8,72},{12,76},{16,80},{20,84},{24,88},{28,92},{32,9... | collective-permute-start | bytes 294920 | tf_op jit(solution)/shard_map/ppermute | solution.py:364
  24.2 5.8 %collective-permute-start.5 = (f32[8,3072]{1,0:T(8,128)S(1)}, f32[8,3072]{1,0:T(8,128)S(1)}, u32[]{:S(2)}, u32[]{:S(2)}) collective-permute-start(f32[8,3072]{1,0:T(8,128)S(1)} %add_add_fusion.refs_0_), channel_id=1, source_target_pairs={{0,96},{4,100},{8,104},{12,108},{16,112},{20,116},{24,120},{28,124... | collective-permute-start | bytes 294920 | tf_op jit(solution)/shard_map/ppermute | solution.py:364
  25.2 4.8 %collective-permute-start.4 = (f32[8,3072]{1,0:T(8,128)S(1)}, f32[8,3072]{1,0:T(8,128)S(1)}, u32[]{:S(2)}, u32[]{:S(2)}) collective-permute-start(f32[8,3072]{1,0:T(8,128)S(1)} %add_add_fusion.refs_0_), channel_id=1, source_target_pairs={{0,32},{4,36},{8,40},{12,44},{16,48},{20,52},{24,56},{28,60},{32,0... | collective-permute-start | bytes 294920 | tf_op jit(solution)/shard_map/ppermute | solution.py:364
  25.2 14.2 %collective-permute-start.11 = (bf16[384,1024]{1,0:T(8,128)(2,1)S(1)}, bf16[384,1024]{1,0:T(8,128)(2,1)S(1)}, u32[]{:S(2)}, u32[]{:S(2)}) collective-permute-start(bf16[384,1024]{1,0:T(8,128)(2,1)S(1)} %get-tuple-element.49), channel_id=1, source_target_pairs={{1,0},{2,1},{3,2},{0,3},{5,4},{6,5},{7,6},{4,7},{9,8},{10,9},{11,1... | collective-permute-start | bytes 2359304 | tf_op jit(solution)/shard_map/ppermute | solution.py:372
  31.9 5.8 %collective-permute-start.10 = (bf16[8,3072]{1,0:T(8,128)(2,1)S(1)}, bf16[8,3072]{1,0:T(8,128)(2,1)S(1)}, u32[]{:S(2)}, u32[]{:S(2)}) collective-permute-start(bf16[8,3072]{1,0:T(8,128)(2,1)S(1)} %get-tuple-element.46), channel_id=1, source_target_pairs={{0,8},{4,12},{8,0},{12,4},{16,24},{20,28},{24,16},{28,20},{32,40},... | collective-permute-start | bytes 147464 | tf_op jit(solution)/shard_map/ppermute | solution.py:364
  34.1 5.3 %collective-permute-start.9 = (bf16[8,3072]{1,0:T(8,128)(2,1)S(1)}, bf16[8,3072]{1,0:T(8,128)(2,1)S(1)}, u32[]{:S(2)}, u32[]{:S(2)}) collective-permute-start(bf16[8,3072]{1,0:T(8,128)(2,1)S(1)} %get-tuple-element.46), channel_id=1, source_target_pairs={{0,12},{4,8},{8,4},{12,0},{16,28},{20,24},{24,20},{28,16},{32,44},... | collective-permute-start | bytes 147464 | tf_op jit(solution)/shard_map/ppermute | solution.py:364
  35.3 4.2 %collective-permute-start.8 = (bf16[8,3072]{1,0:T(8,128)(2,1)S(1)}, bf16[8,3072]{1,0:T(8,128)(2,1)S(1)}, u32[]{:S(2)}, u32[]{:S(2)}) collective-permute-start(bf16[8,3072]{1,0:T(8,128)(2,1)S(1)} %get-tuple-element.46), channel_id=1, source_target_pairs={{0,4},{4,0},{8,12},{12,8},{16,20},{20,16},{24,28},{28,24},{32,36},... | collective-permute-start | bytes 147464 | tf_op jit(solution)/shard_map/ppermute | solution.py:364
  35.5 12.1 %collective-permute-start.15 = (bf16[384,1024]{1,0:T(8,128)(2,1)S(1)}, bf16[384,1024]{1,0:T(8,128)(2,1)S(1)}, u32[]{:S(2)}, u32[]{:S(2)}) collective-permute-start(bf16[384,1024]{1,0:T(8,128)(2,1)S(1)} %product_part.5), channel_id=1, source_target_pairs={{1,0},{2,1},{3,2},{0,3},{5,4},{6,5},{7,6},{4,7},{9,8},{10,9},{11,1... | collective-permute-start | bytes 2359304 | tf_op jit(solution)/shard_map/ppermute | solution.py:372
  39.5 6.1 %collective-permute-start.14 = (bf16[8,3072]{1,0:T(8,128)(2,1)S(1)}, bf16[8,3072]{1,0:T(8,128)(2,1)S(1)}, u32[]{:S(2)}, u32[]{:S(2)}) collective-permute-start(bf16[8,3072]{1,0:T(8,128)(2,1)S(1)} %add_convert_fusion.1), channel_id=1, source_target_pairs={{0,64},{4,68},{8,72},{12,76},{16,80},{20,84},{24,88},{28,92},{32,9... | collective-permute-start | bytes 147464 | tf_op jit(solution)/shard_map/ppermute | solution.py:364
  41.4 5.3 %collective-permute-start.13 = (bf16[8,3072]{1,0:T(8,128)(2,1)S(1)}, bf16[8,3072]{1,0:T(8,128)(2,1)S(1)}, u32[]{:S(2)}, u32[]{:S(2)}) collective-permute-start(bf16[8,3072]{1,0:T(8,128)(2,1)S(1)} %add_convert_fusion.1), channel_id=1, source_target_pairs={{0,96},{4,100},{8,104},{12,108},{16,112},{20,116},{24,120},{28,124... | collective-permute-start | bytes 147464 | tf_op jit(solution)/shard_map/ppermute | solution.py:364
  43.4 4.1 %collective-permute-start.12 = (bf16[8,3072]{1,0:T(8,128)(2,1)S(1)}, bf16[8,3072]{1,0:T(8,128)(2,1)S(1)}, u32[]{:S(2)}, u32[]{:S(2)}) collective-permute-start(bf16[8,3072]{1,0:T(8,128)(2,1)S(1)} %add_convert_fusion.1), channel_id=1, source_target_pairs={{0,32},{4,36},{8,40},{12,44},{16,48},{20,52},{24,56},{28,60},{32,0... | collective-permute-start | bytes 147464 | tf_op jit(solution)/shard_map/ppermute | solution.py:364
  47.6 5.7 %collective-permute-start.16 = (bf16[8,3072]{1,0:T(8,128)(2,1)S(1)}, bf16[8,3072]{1,0:T(8,128)(2,1)S(1)}, u32[]{:S(2)}, u32[]{:S(2)}) collective-permute-start(bf16[8,3072]{1,0:T(8,128)(2,1)S(1)} %add_convert_fusion), channel_id=1, source_target_pairs={{0,16},{4,20},{8,24},{12,28},{16,0},{20,4},{24,8},{28,12},{32,48},... | collective-permute-start | bytes 147464 | tf_op jit(solution)/shard_map/ppermute | solution.py:364

commit v4 on v3

--- a/solution.py
+++ b/solution.py
@@ -355,7 +355,11 @@
 X_ROUND = swaps((0, 1, 0))
 Y_ROUND = swaps((1, 0, 0), (3, 0, 0), (2, 0, 0))
 Z_ROUND = swaps((0, 0, 1), (0, 0, 3), (0, 0, 2))
-LEFT_ROUNDS = [X_ROUND, Z_ROUND, Y_ROUND]
+LEFT_ROUNDS = [
+    X_ROUND,
+    swaps((0, 0, 3), (0, 0, 1), (0, 0, 2)),
+    swaps((3, 0, 0), (1, 0, 0), (2, 0, 0)),
+]
 PART_OF_ROUND = {0: 0, 1: 1, 2: 2}
 RIGHT_ROUNDS = [Z_ROUND, Y_ROUND, X_ROUND]
 

time: 54 us -> 53.9 us (level)
  transfers between devices with their start and end apart: 17 -> 17, of which waited for: 8 -> 11; matrix products, arithmetic and copies ran while one was open for 0% -> 0% of each run, Pallas kernels for 25% -> 25%
where the time goes in v4:
time: 53.9 us; the launch traced here: 53.7 us
  starting transfers between devices  22 us (41%)
  Pallas kernels  16.8 us (31%)
  waiting for transfers between devices  13.4 us (25%)
  between operations  0.76 us (1%)
  other arithmetic  0.74 us (1%)
    ppermute x14, starting transfers between devices, sent(): return [lax.ppermute(value, 'dp', pairs) for pairs in pattern]  22 us
    ppermute x14, waiting for transfers between devices, sent(): return [lax.ppermute(value, 'dp', pairs) for pairs in pattern]  13.4 us
    pallas_call x3, Pallas kernels, product_part(): pl.pallas_call(functools.partial(product_kernel, base, sizes, ahead), out...  9.34 us
    pallas_call x1, Pallas kernels, first_products(): pl.pallas_call(first_kernel, out_shape=out_shape, in_specs=[anywhere()] *...  3.43 us
    pallas_call x1, Pallas kernels, second_products(): pl.pallas_call(second_kernel, out_shape=(VMEM((RANK, D_IN), F32), VMEM((R...  1.91 us
    pallas_call x1, Pallas kernels, stored(): pl.pallas_call(store_kernel, out_shape=jax.ShapeDtypeStruct((TOKENS, D_IN...  1.45 us
  transfers between devices with their start and end apart: 17, of which 11 were waited for; matrix products, arithmetic and copies ran while one was open for 0% of the time, Pallas kernels for 25%

profile of v4, /device:TPU:0, one launch (start us, length us, event | category | flops | bytes accessed | tf_op | source)
XLA Modules:
  0.0 53.7 jit_solution(13224722806903727761)
XLA Ops:
  0.6 3.4 %first_products.1 = (f32[8,3072]{1,0:T(8,128)S(1)}, bf16[384,3072]{1,0:T(8,128)(2,1)S(1)}, bf16[384,3072]{1,0:T(8,128)(2,1)S(1)}, bf16[512,3072]{1,0:T(8,128)(2,1)S(1)}) custom-call(bf16[8,3072]{1,0:T(8,128)(2,1)} %bitcast.16, bf16[384,3072]{1,0:T(8,128)(2,1)} %bitcast.12, bf16[384,3072]{1,0:T(8,128)(2,1)} %bitcast.13, bf16[3072,3072]{1,0:T(8,128)(2,1)} %bitcast.8), custom_call_target="tpu_custom_call" | custom-call | flops 150994944 | bytes 4718592 | tf_op jit(solution)/shard_map/first_products/pallas_call | solution.py:118
  4.1 3.2 %collective-permute-start = (f32[8,3072]{1,0:T(8,128)S(1)}, f32[8,3072]{1,0:T(8,128)S(1)}, u32[]{:S(2)}, u32[]{:S(2)}) collective-permute-start(f32[8,3072]{1,0:T(8,128)S(1)} %get-tuple-element.31), channel_id=1, source_target_pairs={{0,16},{4,20},{8,24},{12,28},{16,0},{20,4},{24,8},{28,12},{32,48},... | collective-permute-start | bytes 294920 | tf_op jit(solution)/shard_map/ppermute | solution.py:368
  7.3 3.8 %product_part.3 = (bf16[384,1024]{1,0:T(8,128)(2,1)S(1)}, bf16[1024,3072]{1,0:T(8,128)(2,1)S(1)}) custom-call(bf16[384,3072]{1,0:T(8,128)(2,1)S(1)} %get-tuple-element.32.grads_ref.refs_4_, bf16[512,3072]{1,0:T(8,128)(2,1)S(1)} %get-tuple-element.33.refs_0_, bf16[3072,3072]{1,0:T(8,128)(2,1)} %bitcast.9), custom_call_target="tpu_custom_call" | custom-call | flops 603979776 | bytes 1572864 | tf_op jit(solution)/shard_map/product_part/pallas_call | solution.py:267
  11.1 0.0 collective-permute-done
  11.1 4.0 %collective-permute-start.3 = (f32[8,3072]{1,0:T(8,128)S(1)}, f32[8,3072]{1,0:T(8,128)S(1)}, u32[]{:S(2)}, u32[]{:S(2)}) collective-permute-start(f32[8,3072]{1,0:T(8,128)S(1)} %add.33), channel_id=1, source_target_pairs={{0,8},{4,12},{8,0},{12,4},{16,24},{20,28},{24,16},{28,20},{32,40},... | collective-permute-start | bytes 294920 | tf_op jit(solution)/shard_map/ppermute | solution.py:368
  15.1 1.0 %collective-permute-start.2 = (f32[8,3072]{1,0:T(8,128)S(1)}, f32[8,3072]{1,0:T(8,128)S(1)}, u32[]{:S(2)}, u32[]{:S(2)}) collective-permute-start(f32[8,3072]{1,0:T(8,128)S(1)} %add.33), channel_id=1, source_target_pairs={{0,4},{4,0},{8,12},{12,8},{16,20},{20,16},{24,28},{28,24},{32,36},... | collective-permute-start | bytes 294920 | tf_op jit(solution)/shard_map/ppermute | solution.py:368
  16.1 0.0 collective-permute-start.1
  16.1 0.0 collective-permute-start.7
  16.1 2.8 %product_part.4 = (bf16[384,1024]{1,0:T(8,128)(2,1)S(1)}, bf16[1024,3072]{1,0:T(8,128)(2,1)S(1)}) custom-call(bf16[384,3072]{1,0:T(8,128)(2,1)S(1)} %get-tuple-element.32.grads_ref.refs_4_, bf16[1024,3072]{1,0:T(8,128)(2,1)S(1)} %get-tuple-element.36.refs_0_, bf16[3072,3072]{1,0:T(8,128)(2,1)} %bitcast.10), custom_call_target="tpu_custom_call" | custom-call | flops 603979776 | bytes 1572864 | tf_op jit(solution)/shard_map/product_part/pallas_call | solution.py:267
  18.9 0.0 collective-permute-done.3
  18.9 1.5 %collective-permute-done.2 = f32[8,3072]{1,0:T(8,128)S(1)} collective-permute-done((f32[8,3072]{1,0:T(8,128)S(1)}, f32[8,3072]{1,0:T(8,128)S(1)}, u32[]{:S(2)}, u32[]{:S(2)}) %collective-permute-start.2) | collective-permute-done | bytes 98336 | tf_op jit(solution)/shard_map/ppermute | solution.py:368
  20.4 1.5 %collective-permute-done.1 = f32[8,3072]{1,0:T(8,128)S(1)} collective-permute-done((f32[8,3072]{1,0:T(8,128)S(1)}, f32[8,3072]{1,0:T(8,128)S(1)}, u32[]{:S(2)}, u32[]{:S(2)}) %collective-permute-start.1) | collective-permute-done | bytes 98336 | tf_op jit(solution)/shard_map/ppermute | solution.py:368
  21.9 3.3 %collective-permute-start.6 = (f32[8,3072]{1,0:T(8,128)S(1)}, f32[8,3072]{1,0:T(8,128)S(1)}, u32[]{:S(2)}, u32[]{:S(2)}) collective-permute-start(f32[8,3072]{1,0:T(8,128)S(1)} %add_add_fusion.refs_0_), channel_id=1, source_target_pairs={{0,64},{4,68},{8,72},{12,76},{16,80},{20,84},{24,88},{28,92},{32,9... | collective-permute-start | bytes 294920 | tf_op jit(solution)/shard_map/ppermute | solution.py:368
  25.2 0.7 %collective-permute-start.5 = (f32[8,3072]{1,0:T(8,128)S(1)}, f32[8,3072]{1,0:T(8,128)S(1)}, u32[]{:S(2)}, u32[]{:S(2)}) collective-permute-start(f32[8,3072]{1,0:T(8,128)S(1)} %add_add_fusion.refs_0_), channel_id=1, source_target_pairs={{0,32},{4,36},{8,40},{12,44},{16,48},{20,52},{24,56},{28,60},{32,0... | collective-permute-start | bytes 294920 | tf_op jit(solution)/shard_map/ppermute | solution.py:368
  25.9 0.4 collective-permute-start.4
  26.3 0.0 collective-permute-start.11
  26.3 2.7 %product_part.5 = bf16[384,1024]{1,0:T(8,128)(2,1)S(1)} custom-call(bf16[384,3072]{1,0:T(8,128)(2,1)S(1)} %get-tuple-element.32.grads_ref.refs_4_, bf16[1024,3072]{1,0:T(8,128)(2,1)S(1)} %get-tuple-element.40.refs_0_, bf16[3072,3072]{1,0:T(8,128)(2,1)} %bitcast.11), custom_call_target="tpu_custom_call" | custom-call | flops 603979776 | bytes 1572864 | tf_op jit(solution)/shard_map/product_part/pallas_call | solution.py:267
  29.0 0.0 collective-permute-done.6.refs_3_
  29.0 0.8 %collective-permute-done.5.refs_2_ = f32[8,3072]{1,0:T(8,128)S(1)} collective-permute-done((f32[8,3072]{1,0:T(8,128)S(1)}, f32[8,3072]{1,0:T(8,128)S(1)}, u32[]{:S(2)}, u32[]{:S(2)}) %collective-permute-start.5) | collective-permute-done | bytes 98336 | tf_op jit(solution)/shard_map/ppermute | solution.py:368
  29.8 1.9 %collective-permute-done.4.refs_1_ = f32[8,3072]{1,0:T(8,128)S(1)} collective-permute-done((f32[8,3072]{1,0:T(8,128)S(1)}, f32[8,3072]{1,0:T(8,128)S(1)}, u32[]{:S(2)}, u32[]{:S(2)}) %collective-permute-start.4) | collective-permute-done | bytes 98336 | tf_op jit(solution)/shard_map/ppermute | solution.py:368
  31.7 0.0 collective-permute-done.7.refs_0_
  31.7 1.9 %second_products.1 = (f32[8,3072]{1,0:T(8,128)S(1)}, bf16[8,3072]{1,0:T(8,128)(2,1)S(1)}) custom-call(f32[8,3072]{1,0:T(8,128)S(1)} %add_add_fusion.refs_0_, f32[8,3072]{1,0:T(8,128)S(1)} %collective-permute-done.4.refs_1_, f32[8,3072]{1,0:T(8,128)S(1)} %collective-permute-done.5.refs_2_, f32[8,3072]{1,0:T(8,128)S(1)} %collective-permute-done.6.refs_3_, ...), custom_call_target="tpu_custom_call" | custom-call | flops 150994944 | bytes 589824 | tf_op jit(solution)/shard_map/second_products/pallas_call | solution.py:178
  33.6 1.1 %collective-permute-start.10 = (bf16[8,3072]{1,0:T(8,128)(2,1)S(1)}, bf16[8,3072]{1,0:T(8,128)(2,1)S(1)}, u32[]{:S(2)}, u32[]{:S(2)}) collective-permute-start(bf16[8,3072]{1,0:T(8,128)(2,1)S(1)} %get-tuple-element.46), channel_id=1, source_target_pairs={{0,8},{4,12},{8,0},{12,4},{16,24},{20,28},{24,16},{28,20},{32,40},... | collective-permute-start | bytes 147464 | tf_op jit(solution)/shard_map/ppermute | solution.py:368
  34.7 1.4 %collective-permute-start.9 = (bf16[8,3072]{1,0:T(8,128)(2,1)S(1)}, bf16[8,3072]{1,0:T(8,128)(2,1)S(1)}, u32[]{:S(2)}, u32[]{:S(2)}) collective-permute-start(bf16[8,3072]{1,0:T(8,128)(2,1)S(1)} %get-tuple-element.46), channel_id=1, source_target_pairs={{0,12},{4,8},{8,4},{12,0},{16,28},{20,24},{24,20},{28,16},{32,44},... | collective-permute-start | bytes 147464 | tf_op jit(solution)/shard_map/ppermute | solution.py:368
  36.2 1.0 %collective-permute-start.8 = (bf16[8,3072]{1,0:T(8,128)(2,1)S(1)}, bf16[8,3072]{1,0:T(8,128)(2,1)S(1)}, u32[]{:S(2)}, u32[]{:S(2)}) collective-permute-start(bf16[8,3072]{1,0:T(8,128)(2,1)S(1)} %get-tuple-element.46), channel_id=1, source_target_pairs={{0,4},{4,0},{8,12},{12,8},{16,20},{20,16},{24,28},{28,24},{32,36},... | collective-permute-start | bytes 147464 | tf_op jit(solution)/shard_map/ppermute | solution.py:368
  37.2 0.0 collective-permute-start.15
  37.2 0.6 %left_stored.1 = f32[8,3072]{1,0:T(8,128)} custom-call(f32[8,3072]{1,0:T(8,128)S(1)} %get-tuple-element.47.left_ref), custom_call_target="tpu_custom_call" | custom-call | tf_op jit(solution)/shard_map/left_stored/pallas_call | solution.py:198
  37.9 1.4 %collective-permute-done.10 = bf16[8,3072]{1,0:T(8,128)(2,1)S(1)} collective-permute-done((bf16[8,3072]{1,0:T(8,128)(2,1)S(1)}, bf16[8,3072]{1,0:T(8,128)(2,1)S(1)}, u32[]{:S(2)}, u32[]{:S(2)}) %collective-permute-start.10) | collective-permute-done | bytes 49184 | tf_op jit(solution)/shard_map/ppermute | solution.py:368
  39.3 0.7 %collective-permute-done.9 = bf16[8,3072]{1,0:T(8,128)(2,1)S(1)} collective-permute-done((bf16[8,3072]{1,0:T(8,128)(2,1)S(1)}, bf16[8,3072]{1,0:T(8,128)(2,1)S(1)}, u32[]{:S(2)}, u32[]{:S(2)}) %collective-permute-start.9) | collective-permute-done | bytes 49184 | tf_op jit(solution)/shard_map/ppermute | solution.py:368
  40.0 0.2 collective-permute-done.8
  40.3 0.0 collective-permute-done.11.refs_1_
  40.3 1.3 %collective-permute-start.14 = (bf16[8,3072]{1,0:T(8,128)(2,1)S(1)}, bf16[8,3072]{1,0:T(8,128)(2,1)S(1)}, u32[]{:S(2)}, u32[]{:S(2)}) collective-permute-start(bf16[8,3072]{1,0:T(8,128)(2,1)S(1)} %add_convert_fusion.1), channel_id=1, source_target_pairs={{0,64},{4,68},{8,72},{12,76},{16,80},{20,84},{24,88},{28,92},{32,9... | collective-permute-start | bytes 147464 | tf_op jit(solution)/shard_map/ppermute | solution.py:368
  41.6 1.6 %collective-permute-start.13 = (bf16[8,3072]{1,0:T(8,128)(2,1)S(1)}, bf16[8,3072]{1,0:T(8,128)(2,1)S(1)}, u32[]{:S(2)}, u32[]{:S(2)}) collective-permute-start(bf16[8,3072]{1,0:T(8,128)(2,1)S(1)} %add_convert_fusion.1), channel_id=1, source_target_pairs={{0,96},{4,100},{8,104},{12,108},{16,112},{20,116},{24,120},{28,124... | collective-permute-start | bytes 147464 | tf_op jit(solution)/shard_map/ppermute | solution.py:368
  43.2 0.7 %collective-permute-start.12 = (bf16[8,3072]{1,0:T(8,128)(2,1)S(1)}, bf16[8,3072]{1,0:T(8,128)(2,1)S(1)}, u32[]{:S(2)}, u32[]{:S(2)}) collective-permute-start(bf16[8,3072]{1,0:T(8,128)(2,1)S(1)} %add_convert_fusion.1), channel_id=1, source_target_pairs={{0,32},{4,36},{8,40},{12,44},{16,48},{20,52},{24,56},{28,60},{32,0... | collective-permute-start | bytes 147464 | tf_op jit(solution)/shard_map/ppermute | solution.py:368
  43.9 2.1 %collective-permute-done.14 = bf16[8,3072]{1,0:T(8,128)(2,1)S(1)} collective-permute-done((bf16[8,3072]{1,0:T(8,128)(2,1)S(1)}, bf16[8,3072]{1,0:T(8,128)(2,1)S(1)}, u32[]{:S(2)}, u32[]{:S(2)}) %collective-permute-start.14) | collective-permute-done | bytes 49184 | tf_op jit(solution)/shard_map/ppermute | solution.py:368
  46.0 0.9 %collective-permute-done.13 = bf16[8,3072]{1,0:T(8,128)(2,1)S(1)} collective-permute-done((bf16[8,3072]{1,0:T(8,128)(2,1)S(1)}, bf16[8,3072]{1,0:T(8,128)(2,1)S(1)}, u32[]{:S(2)}, u32[]{:S(2)}) %collective-permute-start.13) | collective-permute-done | bytes 49184 | tf_op jit(solution)/shard_map/ppermute | solution.py:368
  46.9 0.4 collective-permute-done.12
  47.3 0.0 collective-permute-done.15.refs_2_
  47.3 2.4 %collective-permute-start.16 = (bf16[8,3072]{1,0:T(8,128)(2,1)S(1)}, bf16[8,3072]{1,0:T(8,128)(2,1)S(1)}, u32[]{:S(2)}, u32[]{:S(2)}) collective-permute-start(bf16[8,3072]{1,0:T(8,128)(2,1)S(1)} %add_convert_fusion), channel_id=1, source_target_pairs={{0,16},{4,20},{8,24},{12,28},{16,0},{20,4},{24,8},{28,12},{32,48},... | collective-permute-start | bytes 147464 | tf_op jit(solution)/shard_map/ppermute | solution.py:368
  49.7 1.4 %store.1 = bf16[384,3072]{1,0:T(8,128)(2,1)} custom-call(bf16[384,1024]{1,0:T(8,128)(2,1)S(1)} %collective-permute-done.7.refs_0_, bf16[384,1024]{1,0:T(8,128)(2,1)S(1)} %collective-permute-done.11.refs_1_, bf16[384,1024]{1,0:T(8,128)(2,1)S(1)} %collective-permute-done.15.refs_2_), custom_call_target="tpu_custom_call" | custom-call | bytes 4718592 | tf_op jit(solution)/shard_map/store/pallas_call | solution.py:313
  51.2 1.8 %collective-permute-done.16 = bf16[8,3072]{1,0:T(8,128)(2,1)S(1)} collective-permute-done((bf16[8,3072]{1,0:T(8,128)(2,1)S(1)}, bf16[8,3072]{1,0:T(8,128)(2,1)S(1)}, u32[]{:S(2)}, u32[]{:S(2)}) %collective-permute-start.16) | collective-permute-done | bytes 49184 | tf_op jit(solution)/shard_map/ppermute | solution.py:368
  53.0 0.7 %add_bitcast_fusion = f32[1,8,3072]{2,1,0:T(8,128)} fusion(bf16[8,3072]{1,0:T(8,128)(2,1)S(1)} %collective-permute-done.16, bf16[8,3072]{1,0:T(8,128)(2,1)S(1)} %add_convert_fusion), kind=kLoop, calls=%fused_computation | loop fusion | flops 73728 | bytes 196608 | tf_op jit(solution)/shard_map/broadcast_in_dim | solution.py:412
  (4 shorter events, 0.1 us)
Async XLA Ops:
  4.1 7.0 %collective-permute-start = (f32[8,3072]{1,0:T(8,128)S(1)}, f32[8,3072]{1,0:T(8,128)S(1)}, u32[]{:S(2)}, u32[]{:S(2)}) collective-permute-start(f32[8,3072]{1,0:T(8,128)S(1)} %get-tuple-element.31), channel_id=1, source_target_pairs={{0,16},{4,20},{8,24},{12,28},{16,0},{20,4},{24,8},{28,12},{32,48},... | collective-permute-start | bytes 294920 | tf_op jit(solution)/shard_map/ppermute | solution.py:368
  11.1 7.8 %collective-permute-start.3 = (f32[8,3072]{1,0:T(8,128)S(1)}, f32[8,3072]{1,0:T(8,128)S(1)}, u32[]{:S(2)}, u32[]{:S(2)}) collective-permute-start(f32[8,3072]{1,0:T(8,128)S(1)} %add.33), channel_id=1, source_target_pairs={{0,8},{4,12},{8,0},{12,4},{16,24},{20,28},{24,16},{28,20},{32,40},... | collective-permute-start | bytes 294920 | tf_op jit(solution)/shard_map/ppermute | solution.py:368
  15.1 5.4 %collective-permute-start.2 = (f32[8,3072]{1,0:T(8,128)S(1)}, f32[8,3072]{1,0:T(8,128)S(1)}, u32[]{:S(2)}, u32[]{:S(2)}) collective-permute-start(f32[8,3072]{1,0:T(8,128)S(1)} %add.33), channel_id=1, source_target_pairs={{0,4},{4,0},{8,12},{12,8},{16,20},{20,16},{24,28},{28,24},{32,36},... | collective-permute-start | bytes 294920 | tf_op jit(solution)/shard_map/ppermute | solution.py:368
  16.1 5.8 %collective-permute-start.1 = (f32[8,3072]{1,0:T(8,128)S(1)}, f32[8,3072]{1,0:T(8,128)S(1)}, u32[]{:S(2)}, u32[]{:S(2)}) collective-permute-start(f32[8,3072]{1,0:T(8,128)S(1)} %add.33), channel_id=1, source_target_pairs={{0,12},{4,8},{8,4},{12,0},{16,28},{20,24},{24,20},{28,16},{32,44},... | collective-permute-start | bytes 294920 | tf_op jit(solution)/shard_map/ppermute | solution.py:368
  16.1 15.6 %collective-permute-start.7 = (bf16[384,1024]{1,0:T(8,128)(2,1)S(1)}, bf16[384,1024]{1,0:T(8,128)(2,1)S(1)}, u32[]{:S(2)}, u32[]{:S(2)}) collective-permute-start(bf16[384,1024]{1,0:T(8,128)(2,1)S(1)} %get-tuple-element.39), channel_id=1, source_target_pairs={{1,0},{2,1},{3,2},{0,3},{5,4},{6,5},{7,6},{4,7},{9,8},{10,9},{11,1... | collective-permute-start | bytes 2359304 | tf_op jit(solution)/shard_map/ppermute | solution.py:376
  21.9 7.0 %collective-permute-start.6 = (f32[8,3072]{1,0:T(8,128)S(1)}, f32[8,3072]{1,0:T(8,128)S(1)}, u32[]{:S(2)}, u32[]{:S(2)}) collective-permute-start(f32[8,3072]{1,0:T(8,128)S(1)} %add_add_fusion.refs_0_), channel_id=1, source_target_pairs={{0,64},{4,68},{8,72},{12,76},{16,80},{20,84},{24,88},{28,92},{32,9... | collective-permute-start | bytes 294920 | tf_op jit(solution)/shard_map/ppermute | solution.py:368
  25.2 4.6 %collective-permute-start.5 = (f32[8,3072]{1,0:T(8,128)S(1)}, f32[8,3072]{1,0:T(8,128)S(1)}, u32[]{:S(2)}, u32[]{:S(2)}) collective-permute-start(f32[8,3072]{1,0:T(8,128)S(1)} %add_add_fusion.refs_0_), channel_id=1, source_target_pairs={{0,32},{4,36},{8,40},{12,44},{16,48},{20,52},{24,56},{28,60},{32,0... | collective-permute-start | bytes 294920 | tf_op jit(solution)/shard_map/ppermute | solution.py:368
  25.9 5.8 %collective-permute-start.4 = (f32[8,3072]{1,0:T(8,128)S(1)}, f32[8,3072]{1,0:T(8,128)S(1)}, u32[]{:S(2)}, u32[]{:S(2)}) collective-permute-start(f32[8,3072]{1,0:T(8,128)S(1)} %add_add_fusion.refs_0_), channel_id=1, source_target_pairs={{0,96},{4,100},{8,104},{12,108},{16,112},{20,116},{24,120},{28,124... | collective-permute-start | bytes 294920 | tf_op jit(solution)/shard_map/ppermute | solution.py:368
  26.3 14.0 %collective-permute-start.11 = (bf16[384,1024]{1,0:T(8,128)(2,1)S(1)}, bf16[384,1024]{1,0:T(8,128)(2,1)S(1)}, u32[]{:S(2)}, u32[]{:S(2)}) collective-permute-start(bf16[384,1024]{1,0:T(8,128)(2,1)S(1)} %get-tuple-element.49), channel_id=1, source_target_pairs={{1,0},{2,1},{3,2},{0,3},{5,4},{6,5},{7,6},{4,7},{9,8},{10,9},{11,1... | collective-permute-start | bytes 2359304 | tf_op jit(solution)/shard_map/ppermute | solution.py:376
  33.6 5.7 %collective-permute-start.10 = (bf16[8,3072]{1,0:T(8,128)(2,1)S(1)}, bf16[8,3072]{1,0:T(8,128)(2,1)S(1)}, u32[]{:S(2)}, u32[]{:S(2)}) collective-permute-start(bf16[8,3072]{1,0:T(8,128)(2,1)S(1)} %get-tuple-element.46), channel_id=1, source_target_pairs={{0,8},{4,12},{8,0},{12,4},{16,24},{20,28},{24,16},{28,20},{32,40},... | collective-permute-start | bytes 147464 | tf_op jit(solution)/shard_map/ppermute | solution.py:368
  34.7 5.3 %collective-permute-start.9 = (bf16[8,3072]{1,0:T(8,128)(2,1)S(1)}, bf16[8,3072]{1,0:T(8,128)(2,1)S(1)}, u32[]{:S(2)}, u32[]{:S(2)}) collective-permute-start(bf16[8,3072]{1,0:T(8,128)(2,1)S(1)} %get-tuple-element.46), channel_id=1, source_target_pairs={{0,12},{4,8},{8,4},{12,0},{16,28},{20,24},{24,20},{28,16},{32,44},... | collective-permute-start | bytes 147464 | tf_op jit(solution)/shard_map/ppermute | solution.py:368
  36.2 4.1 %collective-permute-start.8 = (bf16[8,3072]{1,0:T(8,128)(2,1)S(1)}, bf16[8,3072]{1,0:T(8,128)(2,1)S(1)}, u32[]{:S(2)}, u32[]{:S(2)}) collective-permute-start(bf16[8,3072]{1,0:T(8,128)(2,1)S(1)} %get-tuple-element.46), channel_id=1, source_target_pairs={{0,4},{4,0},{8,12},{12,8},{16,20},{20,16},{24,28},{28,24},{32,36},... | collective-permute-start | bytes 147464 | tf_op jit(solution)/shard_map/ppermute | solution.py:368
  37.2 10.1 %collective-permute-start.15 = (bf16[384,1024]{1,0:T(8,128)(2,1)S(1)}, bf16[384,1024]{1,0:T(8,128)(2,1)S(1)}, u32[]{:S(2)}, u32[]{:S(2)}) collective-permute-start(bf16[384,1024]{1,0:T(8,128)(2,1)S(1)} %product_part.5), channel_id=1, source_target_pairs={{1,0},{2,1},{3,2},{0,3},{5,4},{6,5},{7,6},{4,7},{9,8},{10,9},{11,1... | collective-permute-start | bytes 2359304 | tf_op jit(solution)/shard_map/ppermute | solution.py:376
  40.3 5.7 %collective-permute-start.14 = (bf16[8,3072]{1,0:T(8,128)(2,1)S(1)}, bf16[8,3072]{1,0:T(8,128)(2,1)S(1)}, u32[]{:S(2)}, u32[]{:S(2)}) collective-permute-start(bf16[8,3072]{1,0:T(8,128)(2,1)S(1)} %add_convert_fusion.1), channel_id=1, source_target_pairs={{0,64},{4,68},{8,72},{12,76},{16,80},{20,84},{24,88},{28,92},{32,9... | collective-permute-start | bytes 147464 | tf_op jit(solution)/shard_map/ppermute | solution.py:368
  41.6 5.3 %collective-permute-start.13 = (bf16[8,3072]{1,0:T(8,128)(2,1)S(1)}, bf16[8,3072]{1,0:T(8,128)(2,1)S(1)}, u32[]{:S(2)}, u32[]{:S(2)}) collective-permute-start(bf16[8,3072]{1,0:T(8,128)(2,1)S(1)} %add_convert_fusion.1), channel_id=1, source_target_pairs={{0,96},{4,100},{8,104},{12,108},{16,112},{20,116},{24,120},{28,124... | collective-permute-start | bytes 147464 | tf_op jit(solution)/shard_map/ppermute | solution.py:368
  43.2 4.1 %collective-permute-start.12 = (bf16[8,3072]{1,0:T(8,128)(2,1)S(1)}, bf16[8,3072]{1,0:T(8,128)(2,1)S(1)}, u32[]{:S(2)}, u32[]{:S(2)}) collective-permute-start(bf16[8,3072]{1,0:T(8,128)(2,1)S(1)} %add_convert_fusion.1), channel_id=1, source_target_pairs={{0,32},{4,36},{8,40},{12,44},{16,48},{20,52},{24,56},{28,60},{32,0... | collective-permute-start | bytes 147464 | tf_op jit(solution)/shard_map/ppermute | solution.py:368
  47.3 5.7 %collective-permute-start.16 = (bf16[8,3072]{1,0:T(8,128)(2,1)S(1)}, bf16[8,3072]{1,0:T(8,128)(2,1)S(1)}, u32[]{:S(2)}, u32[]{:S(2)}) collective-permute-start(bf16[8,3072]{1,0:T(8,128)(2,1)S(1)} %add_convert_fusion), channel_id=1, source_target_pairs={{0,16},{4,20},{8,24},{12,28},{16,0},{20,4},{24,8},{28,12},{32,48},... | collective-permute-start | bytes 147464 | tf_op jit(solution)/shard_map/ppermute | solution.py:368

commit v5 on v4

--- a/solution.py
+++ b/solution.py
@@ -393,7 +393,7 @@
             piece, *held = product_part(grads, held, weight, part)
             held = held[0] if held else piece
             arrived.append(handed(piece))
-    *pieces, arrived[0], _ = tied(value, *arrivals, arrived[0], held)
+    *pieces, _ = tied(value, *arrivals, held)
     left, value = second_products(pieces, grads, inputs)
 
     for place, pattern in enumerate(RIGHT_ROUNDS):

time: 53.9 us -> 60.3 us (1.12)
  waiting for transfers between devices: 13.4 us -> 17.8 us
  starting transfers between devices: 22 us -> 23.4 us
    ppermute x3, waiting for transfers between devices: 0.01 us -> 3.9 us  [handed(): return lax.ppermute(piece, 'section', [(1, 0), (2, 1), (3, 2), (0, 3)])]
    ppermute x3, starting transfers between devices: 0.01 us -> 0.88 us  [handed(): return lax.ppermute(piece, 'section', [(1, 0), (2, 1), (3, 2), (0, 3)])]
  transfers between devices with their start and end apart: 17 -> 17, of which waited for: 11 -> 10; matrix products, arithmetic and copies ran while one was open for 0% -> 0% of each run, Pallas kernels for 25% -> 22%
where the time goes in v5:
time: 60.3 us; the launch traced here: 59.5 us
  starting transfers between devices  23.4 us (39%)
  waiting for transfers between devices  17.8 us (30%)
  Pallas kernels  16.8 us (28%)
  between operations  0.77 us (1%)
  other arithmetic  0.74 us (1%)
    ppermute x14, starting transfers between devices, sent(): return [lax.ppermute(value, 'dp', pairs) for pairs in pattern]  22.5 us
    ppermute x14, waiting for transfers between devices, sent(): return [lax.ppermute(value, 'dp', pairs) for pairs in pattern]  13.9 us
    pallas_call x3, Pallas kernels, product_part(): pl.pallas_call(functools.partial(product_kernel, base, sizes, ahead), out...  9.34 us
    ppermute x3, waiting for transfers between devices, handed(): return lax.ppermute(piece, 'section', [(1, 0), (2, 1), (3, 2), (0, 3)])  3.9 us
    pallas_call x1, Pallas kernels, first_products(): pl.pallas_call(first_kernel, out_shape=out_shape, in_specs=[anywhere()] *...  3.43 us
    pallas_call x1, Pallas kernels, second_products(): pl.pallas_call(second_kernel, out_shape=(VMEM((RANK, D_IN), F32), VMEM((R...  1.9 us
    pallas_call x1, Pallas kernels, stored(): pl.pallas_call(store_kernel, out_shape=jax.ShapeDtypeStruct((TOKENS, D_IN...  1.45 us
  transfers between devices with their start and end apart: 17, of which 10 were waited for; matrix products, arithmetic and copies ran while one was open for 0% of the time, Pallas kernels for 22%

profile of v5, /device:TPU:0, one launch (start us, length us, event | category | flops | bytes accessed | tf_op | source)
XLA Modules:
  0.0 59.5 jit_solution(8737899998037666015)
XLA Ops:
  0.6 3.4 %first_products.1 = (f32[8,3072]{1,0:T(8,128)S(1)}, bf16[384,3072]{1,0:T(8,128)(2,1)S(1)}, bf16[384,3072]{1,0:T(8,128)(2,1)S(1)}, bf16[512,3072]{1,0:T(8,128)(2,1)S(1)}) custom-call(bf16[8,3072]{1,0:T(8,128)(2,1)} %bitcast.16, bf16[384,3072]{1,0:T(8,128)(2,1)} %bitcast.12, bf16[384,3072]{1,0:T(8,128)(2,1)} %bitcast.13, bf16[3072,3072]{1,0:T(8,128)(2,1)} %bitcast.8), custom_call_target="tpu_custom_call" | custom-call | flops 150994944 | bytes 4718592 | tf_op jit(solution)/shard_map/first_products/pallas_call | solution.py:118
  4.1 3.2 %collective-permute-start = (f32[8,3072]{1,0:T(8,128)S(1)}, f32[8,3072]{1,0:T(8,128)S(1)}, u32[]{:S(2)}, u32[]{:S(2)}) collective-permute-start(f32[8,3072]{1,0:T(8,128)S(1)} %get-tuple-element.30), channel_id=1, source_target_pairs={{0,16},{4,20},{8,24},{12,28},{16,0},{20,4},{24,8},{28,12},{32,48},... | collective-permute-start | bytes 294920 | tf_op jit(solution)/shard_map/ppermute | solution.py:368
  7.3 3.8 %product_part.3 = (bf16[384,1024]{1,0:T(8,128)(2,1)S(1)}, bf16[1024,3072]{1,0:T(8,128)(2,1)S(1)}) custom-call(bf16[384,3072]{1,0:T(8,128)(2,1)S(1)} %get-tuple-element.31.grads_ref.refs_4_, bf16[512,3072]{1,0:T(8,128)(2,1)S(1)} %get-tuple-element.32.refs_0_, bf16[3072,3072]{1,0:T(8,128)(2,1)} %bitcast.9), custom_call_target="tpu_custom_call" | custom-call | flops 603979776 | bytes 1572864 | tf_op jit(solution)/shard_map/product_part/pallas_call | solution.py:267
  11.1 0.0 collective-permute-done
  11.1 4.0 %collective-permute-start.3 = (f32[8,3072]{1,0:T(8,128)S(1)}, f32[8,3072]{1,0:T(8,128)S(1)}, u32[]{:S(2)}, u32[]{:S(2)}) collective-permute-start(f32[8,3072]{1,0:T(8,128)S(1)} %add.33), channel_id=1, source_target_pairs={{0,8},{4,12},{8,0},{12,4},{16,24},{20,28},{24,16},{28,20},{32,40},... | collective-permute-start | bytes 294920 | tf_op jit(solution)/shard_map/ppermute | solution.py:368
  15.1 1.0 %collective-permute-start.2 = (f32[8,3072]{1,0:T(8,128)S(1)}, f32[8,3072]{1,0:T(8,128)S(1)}, u32[]{:S(2)}, u32[]{:S(2)}) collective-permute-start(f32[8,3072]{1,0:T(8,128)S(1)} %add.33), channel_id=1, source_target_pairs={{0,4},{4,0},{8,12},{12,8},{16,20},{20,16},{24,28},{28,24},{32,36},... | collective-permute-start | bytes 294920 | tf_op jit(solution)/shard_map/ppermute | solution.py:368
  16.1 0.0 collective-permute-start.1
  16.1 2.8 %product_part.4 = (bf16[384,1024]{1,0:T(8,128)(2,1)S(1)}, bf16[1024,3072]{1,0:T(8,128)(2,1)S(1)}) custom-call(bf16[384,3072]{1,0:T(8,128)(2,1)S(1)} %get-tuple-element.31.grads_ref.refs_4_, bf16[1024,3072]{1,0:T(8,128)(2,1)S(1)} %get-tuple-element.35.refs_0_, bf16[3072,3072]{1,0:T(8,128)(2,1)} %bitcast.10), custom_call_target="tpu_custom_call" | custom-call | flops 603979776 | bytes 1572864 | tf_op jit(solution)/shard_map/product_part/pallas_call | solution.py:267
  18.9 0.0 collective-permute-done.3
  18.9 1.5 %collective-permute-done.2 = f32[8,3072]{1,0:T(8,128)S(1)} collective-permute-done((f32[8,3072]{1,0:T(8,128)S(1)}, f32[8,3072]{1,0:T(8,128)S(1)}, u32[]{:S(2)}, u32[]{:S(2)}) %collective-permute-start.2) | collective-permute-done | bytes 98336 | tf_op jit(solution)/shard_map/ppermute | solution.py:368
  20.4 1.5 %collective-permute-done.1 = f32[8,3072]{1,0:T(8,128)S(1)} collective-permute-done((f32[8,3072]{1,0:T(8,128)S(1)}, f32[8,3072]{1,0:T(8,128)S(1)}, u32[]{:S(2)}, u32[]{:S(2)}) %collective-permute-start.1) | collective-permute-done | bytes 98336 | tf_op jit(solution)/shard_map/ppermute | solution.py:368
  21.9 3.3 %collective-permute-start.6 = (f32[8,3072]{1,0:T(8,128)S(1)}, f32[8,3072]{1,0:T(8,128)S(1)}, u32[]{:S(2)}, u32[]{:S(2)}) collective-permute-start(f32[8,3072]{1,0:T(8,128)S(1)} %add_add_fusion.refs_0_), channel_id=1, source_target_pairs={{0,64},{4,68},{8,72},{12,76},{16,80},{20,84},{24,88},{28,92},{32,9... | collective-permute-start | bytes 294920 | tf_op jit(solution)/shard_map/ppermute | solution.py:368
  25.2 0.7 %collective-permute-start.5 = (f32[8,3072]{1,0:T(8,128)S(1)}, f32[8,3072]{1,0:T(8,128)S(1)}, u32[]{:S(2)}, u32[]{:S(2)}) collective-permute-start(f32[8,3072]{1,0:T(8,128)S(1)} %add_add_fusion.refs_0_), channel_id=1, source_target_pairs={{0,32},{4,36},{8,40},{12,44},{16,48},{20,52},{24,56},{28,60},{32,0... | collective-permute-start | bytes 294920 | tf_op jit(solution)/shard_map/ppermute | solution.py:368
  25.9 0.4 collective-permute-start.4
  26.3 0.0 collective-permute-start.10
  26.3 0.9 %collective-permute-start.11 = (bf16[384,1024]{1,0:T(8,128)(2,1)S(1)}, bf16[384,1024]{1,0:T(8,128)(2,1)S(1)}, u32[]{:S(2)}, u32[]{:S(2)}) collective-permute-start(bf16[384,1024]{1,0:T(8,128)(2,1)S(1)} %get-tuple-element.47), channel_id=1, source_target_pairs={{1,0},{2,1},{3,2},{0,3},{5,4},{6,5},{7,6},{4,7},{9,8},{10,9},{11,1... | collective-permute-start | bytes 2359304 | tf_op jit(solution)/shard_map/ppermute | solution.py:376
  27.1 2.7 %product_part.5 = bf16[384,1024]{1,0:T(8,128)(2,1)S(1)} custom-call(bf16[384,3072]{1,0:T(8,128)(2,1)S(1)} %get-tuple-element.31.grads_ref.refs_4_, bf16[1024,3072]{1,0:T(8,128)(2,1)S(1)} %get-tuple-element.38.refs_0_, bf16[3072,3072]{1,0:T(8,128)(2,1)} %bitcast.11), custom_call_target="tpu_custom_call" | custom-call | flops 603979776 | bytes 1572864 | tf_op jit(solution)/shard_map/product_part/pallas_call | solution.py:267
  29.8 0.0 collective-permute-done.6.refs_3_
  29.8 0.0 collective-permute-done.5.refs_2_
  29.9 1.9 %collective-permute-done.4.refs_1_ = f32[8,3072]{1,0:T(8,128)S(1)} collective-permute-done((f32[8,3072]{1,0:T(8,128)S(1)}, f32[8,3072]{1,0:T(8,128)S(1)}, u32[]{:S(2)}, u32[]{:S(2)}) %collective-permute-start.4) | collective-permute-done | bytes 98336 | tf_op jit(solution)/shard_map/ppermute | solution.py:368
  31.7 1.9 %second_products.1 = (f32[8,3072]{1,0:T(8,128)S(1)}, bf16[8,3072]{1,0:T(8,128)(2,1)S(1)}) custom-call(f32[8,3072]{1,0:T(8,128)S(1)} %add_add_fusion.refs_0_, f32[8,3072]{1,0:T(8,128)S(1)} %collective-permute-done.4.refs_1_, f32[8,3072]{1,0:T(8,128)S(1)} %collective-permute-done.5.refs_2_, f32[8,3072]{1,0:T(8,128)S(1)} %collective-permute-done.6.refs_3_, ...), custom_call_target="tpu_custom_call" | custom-call | flops 150994944 | bytes 589824 | tf_op jit(solution)/shard_map/second_products/pallas_call | solution.py:178
  33.6 1.1 %collective-permute-start.9 = (bf16[8,3072]{1,0:T(8,128)(2,1)S(1)}, bf16[8,3072]{1,0:T(8,128)(2,1)S(1)}, u32[]{:S(2)}, u32[]{:S(2)}) collective-permute-start(bf16[8,3072]{1,0:T(8,128)(2,1)S(1)} %get-tuple-element.44), channel_id=1, source_target_pairs={{0,8},{4,12},{8,0},{12,4},{16,24},{20,28},{24,16},{28,20},{32,40},... | collective-permute-start | bytes 147464 | tf_op jit(solution)/shard_map/ppermute | solution.py:368
  34.7 1.4 %collective-permute-start.8 = (bf16[8,3072]{1,0:T(8,128)(2,1)S(1)}, bf16[8,3072]{1,0:T(8,128)(2,1)S(1)}, u32[]{:S(2)}, u32[]{:S(2)}) collective-permute-start(bf16[8,3072]{1,0:T(8,128)(2,1)S(1)} %get-tuple-element.44), channel_id=1, source_target_pairs={{0,12},{4,8},{8,4},{12,0},{16,28},{20,24},{24,20},{28,16},{32,44},... | collective-permute-start | bytes 147464 | tf_op jit(solution)/shard_map/ppermute | solution.py:368
  36.2 1.0 %collective-permute-start.7 = (bf16[8,3072]{1,0:T(8,128)(2,1)S(1)}, bf16[8,3072]{1,0:T(8,128)(2,1)S(1)}, u32[]{:S(2)}, u32[]{:S(2)}) collective-permute-start(bf16[8,3072]{1,0:T(8,128)(2,1)S(1)} %get-tuple-element.44), channel_id=1, source_target_pairs={{0,4},{4,0},{8,12},{12,8},{16,20},{20,16},{24,28},{28,24},{32,36},... | collective-permute-start | bytes 147464 | tf_op jit(solution)/shard_map/ppermute | solution.py:368
  37.2 0.6 %left_stored.1 = f32[8,3072]{1,0:T(8,128)} custom-call(f32[8,3072]{1,0:T(8,128)S(1)} %get-tuple-element.45.left_ref), custom_call_target="tpu_custom_call" | custom-call | tf_op jit(solution)/shard_map/left_stored/pallas_call | solution.py:198
  37.8 1.4 %collective-permute-done.9 = bf16[8,3072]{1,0:T(8,128)(2,1)S(1)} collective-permute-done((bf16[8,3072]{1,0:T(8,128)(2,1)S(1)}, bf16[8,3072]{1,0:T(8,128)(2,1)S(1)}, u32[]{:S(2)}, u32[]{:S(2)}) %collective-permute-start.9) | collective-permute-done | bytes 49184 | tf_op jit(solution)/shard_map/ppermute | solution.py:368
  39.3 0.0 collective-permute-start.15
  39.3 0.7 %collective-permute-done.8 = bf16[8,3072]{1,0:T(8,128)(2,1)S(1)} collective-permute-done((bf16[8,3072]{1,0:T(8,128)(2,1)S(1)}, bf16[8,3072]{1,0:T(8,128)(2,1)S(1)}, u32[]{:S(2)}, u32[]{:S(2)}) %collective-permute-start.8) | collective-permute-done | bytes 49184 | tf_op jit(solution)/shard_map/ppermute | solution.py:368
  40.0 0.2 collective-permute-done.7
  40.3 0.0 collective-permute-done.10.refs_0_
  40.3 3.9 %collective-permute-done.11.refs_1_ = bf16[384,1024]{1,0:T(8,128)(2,1)S(1)} collective-permute-done((bf16[384,1024]{1,0:T(8,128)(2,1)S(1)}, bf16[384,1024]{1,0:T(8,128)(2,1)S(1)}, u32[]{:S(2)}, u32[]{:S(2)}) %collective-permute-start.11) | collective-permute-done | bytes 786464 | tf_op jit(solution)/shard_map/ppermute | solution.py:376
  44.2 3.0 %collective-permute-start.14 = (bf16[8,3072]{1,0:T(8,128)(2,1)S(1)}, bf16[8,3072]{1,0:T(8,128)(2,1)S(1)}, u32[]{:S(2)}, u32[]{:S(2)}) collective-permute-start(bf16[8,3072]{1,0:T(8,128)(2,1)S(1)} %add_convert_fusion.1), channel_id=1, source_target_pairs={{0,64},{4,68},{8,72},{12,76},{16,80},{20,84},{24,88},{28,92},{32,9... | collective-permute-start | bytes 147464 | tf_op jit(solution)/shard_map/ppermute | solution.py:368
  47.2 1.1 %collective-permute-start.13 = (bf16[8,3072]{1,0:T(8,128)(2,1)S(1)}, bf16[8,3072]{1,0:T(8,128)(2,1)S(1)}, u32[]{:S(2)}, u32[]{:S(2)}) collective-permute-start(bf16[8,3072]{1,0:T(8,128)(2,1)S(1)} %add_convert_fusion.1), channel_id=1, source_target_pairs={{0,96},{4,100},{8,104},{12,108},{16,112},{20,116},{24,120},{28,124... | collective-permute-start | bytes 147464 | tf_op jit(solution)/shard_map/ppermute | solution.py:368
  48.3 0.0 collective-permute-start.12
  48.3 2.0 %collective-permute-done.14 = bf16[8,3072]{1,0:T(8,128)(2,1)S(1)} collective-permute-done((bf16[8,3072]{1,0:T(8,128)(2,1)S(1)}, bf16[8,3072]{1,0:T(8,128)(2,1)S(1)}, u32[]{:S(2)}, u32[]{:S(2)}) %collective-permute-start.14) | collective-permute-done | bytes 49184 | tf_op jit(solution)/shard_map/ppermute | solution.py:368
  50.3 2.6 %collective-permute-done.13 = bf16[8,3072]{1,0:T(8,128)(2,1)S(1)} collective-permute-done((bf16[8,3072]{1,0:T(8,128)(2,1)S(1)}, bf16[8,3072]{1,0:T(8,128)(2,1)S(1)}, u32[]{:S(2)}, u32[]{:S(2)}) %collective-permute-start.13) | collective-permute-done | bytes 49184 | tf_op jit(solution)/shard_map/ppermute | solution.py:368
  52.8 0.0 collective-permute-done.12
  52.9 0.0 collective-permute-done.15.refs_2_
  52.9 2.4 %collective-permute-start.16 = (bf16[8,3072]{1,0:T(8,128)(2,1)S(1)}, bf16[8,3072]{1,0:T(8,128)(2,1)S(1)}, u32[]{:S(2)}, u32[]{:S(2)}) collective-permute-start(bf16[8,3072]{1,0:T(8,128)(2,1)S(1)} %add_convert_fusion), channel_id=1, source_target_pairs={{0,16},{4,20},{8,24},{12,28},{16,0},{20,4},{24,8},{28,12},{32,48},... | collective-permute-start | bytes 147464 | tf_op jit(solution)/shard_map/ppermute | solution.py:368
  55.3 1.4 %store.1 = bf16[384,3072]{1,0:T(8,128)(2,1)} custom-call(bf16[384,1024]{1,0:T(8,128)(2,1)S(1)} %collective-permute-done.10.refs_0_, bf16[384,1024]{1,0:T(8,128)(2,1)S(1)} %collective-permute-done.11.refs_1_, bf16[384,1024]{1,0:T(8,128)(2,1)S(1)} %collective-permute-done.15.refs_2_), custom_call_target="tpu_custom_call" | custom-call | bytes 4718592 | tf_op jit(solution)/shard_map/store/pallas_call | solution.py:313
  56.7 2.1 %collective-permute-done.16 = bf16[8,3072]{1,0:T(8,128)(2,1)S(1)} collective-permute-done((bf16[8,3072]{1,0:T(8,128)(2,1)S(1)}, bf16[8,3072]{1,0:T(8,128)(2,1)S(1)}, u32[]{:S(2)}, u32[]{:S(2)}) %collective-permute-start.16) | collective-permute-done | bytes 49184 | tf_op jit(solution)/shard_map/ppermute | solution.py:368
  58.8 0.7 %add_bitcast_fusion = f32[1,8,3072]{2,1,0:T(8,128)} fusion(bf16[8,3072]{1,0:T(8,128)(2,1)S(1)} %collective-permute-done.16, bf16[8,3072]{1,0:T(8,128)(2,1)S(1)} %add_convert_fusion), kind=kLoop, calls=%fused_computation | loop fusion | flops 73728 | bytes 196608 | tf_op jit(solution)/shard_map/broadcast_in_dim | solution.py:412
  (4 shorter events, 0.1 us)
Async XLA Ops:
  4.1 7.0 %collective-permute-start = (f32[8,3072]{1,0:T(8,128)S(1)}, f32[8,3072]{1,0:T(8,128)S(1)}, u32[]{:S(2)}, u32[]{:S(2)}) collective-permute-start(f32[8,3072]{1,0:T(8,128)S(1)} %get-tuple-element.30), channel_id=1, source_target_pairs={{0,16},{4,20},{8,24},{12,28},{16,0},{20,4},{24,8},{28,12},{32,48},... | collective-permute-start | bytes 294920 | tf_op jit(solution)/shard_map/ppermute | solution.py:368
  11.1 7.8 %collective-permute-start.3 = (f32[8,3072]{1,0:T(8,128)S(1)}, f32[8,3072]{1,0:T(8,128)S(1)}, u32[]{:S(2)}, u32[]{:S(2)}) collective-permute-start(f32[8,3072]{1,0:T(8,128)S(1)} %add.33), channel_id=1, source_target_pairs={{0,8},{4,12},{8,0},{12,4},{16,24},{20,28},{24,16},{28,20},{32,40},... | collective-permute-start | bytes 294920 | tf_op jit(solution)/shard_map/ppermute | solution.py:368
  15.1 5.4 %collective-permute-start.2 = (f32[8,3072]{1,0:T(8,128)S(1)}, f32[8,3072]{1,0:T(8,128)S(1)}, u32[]{:S(2)}, u32[]{:S(2)}) collective-permute-start(f32[8,3072]{1,0:T(8,128)S(1)} %add.33), channel_id=1, source_target_pairs={{0,4},{4,0},{8,12},{12,8},{16,20},{20,16},{24,28},{28,24},{32,36},... | collective-permute-start | bytes 294920 | tf_op jit(solution)/shard_map/ppermute | solution.py:368
  16.1 5.8 %collective-permute-start.1 = (f32[8,3072]{1,0:T(8,128)S(1)}, f32[8,3072]{1,0:T(8,128)S(1)}, u32[]{:S(2)}, u32[]{:S(2)}) collective-permute-start(f32[8,3072]{1,0:T(8,128)S(1)} %add.33), channel_id=1, source_target_pairs={{0,12},{4,8},{8,4},{12,0},{16,28},{20,24},{24,20},{28,16},{32,44},... | collective-permute-start | bytes 294920 | tf_op jit(solution)/shard_map/ppermute | solution.py:368
  21.9 7.9 %collective-permute-start.6 = (f32[8,3072]{1,0:T(8,128)S(1)}, f32[8,3072]{1,0:T(8,128)S(1)}, u32[]{:S(2)}, u32[]{:S(2)}) collective-permute-start(f32[8,3072]{1,0:T(8,128)S(1)} %add_add_fusion.refs_0_), channel_id=1, source_target_pairs={{0,64},{4,68},{8,72},{12,76},{16,80},{20,84},{24,88},{28,92},{32,9... | collective-permute-start | bytes 294920 | tf_op jit(solution)/shard_map/ppermute | solution.py:368
  25.2 4.6 %collective-permute-start.5 = (f32[8,3072]{1,0:T(8,128)S(1)}, f32[8,3072]{1,0:T(8,128)S(1)}, u32[]{:S(2)}, u32[]{:S(2)}) collective-permute-start(f32[8,3072]{1,0:T(8,128)S(1)} %add_add_fusion.refs_0_), channel_id=1, source_target_pairs={{0,32},{4,36},{8,40},{12,44},{16,48},{20,52},{24,56},{28,60},{32,0... | collective-permute-start | bytes 294920 | tf_op jit(solution)/shard_map/ppermute | solution.py:368
  25.9 5.8 %collective-permute-start.4 = (f32[8,3072]{1,0:T(8,128)S(1)}, f32[8,3072]{1,0:T(8,128)S(1)}, u32[]{:S(2)}, u32[]{:S(2)}) collective-permute-start(f32[8,3072]{1,0:T(8,128)S(1)} %add_add_fusion.refs_0_), channel_id=1, source_target_pairs={{0,96},{4,100},{8,104},{12,108},{16,112},{20,116},{24,120},{28,124... | collective-permute-start | bytes 294920 | tf_op jit(solution)/shard_map/ppermute | solution.py:368
  26.3 14.0 %collective-permute-start.10 = (bf16[384,1024]{1,0:T(8,128)(2,1)S(1)}, bf16[384,1024]{1,0:T(8,128)(2,1)S(1)}, u32[]{:S(2)}, u32[]{:S(2)}) collective-permute-start(bf16[384,1024]{1,0:T(8,128)(2,1)S(1)} %get-tuple-element.46), channel_id=1, source_target_pairs={{1,0},{2,1},{3,2},{0,3},{5,4},{6,5},{7,6},{4,7},{9,8},{10,9},{11,1... | collective-permute-start | bytes 2359304 | tf_op jit(solution)/shard_map/ppermute | solution.py:376
  26.3 17.9 %collective-permute-start.11 = (bf16[384,1024]{1,0:T(8,128)(2,1)S(1)}, bf16[384,1024]{1,0:T(8,128)(2,1)S(1)}, u32[]{:S(2)}, u32[]{:S(2)}) collective-permute-start(bf16[384,1024]{1,0:T(8,128)(2,1)S(1)} %get-tuple-element.47), channel_id=1, source_target_pairs={{1,0},{2,1},{3,2},{0,3},{5,4},{6,5},{7,6},{4,7},{9,8},{10,9},{11,1... | collective-permute-start | bytes 2359304 | tf_op jit(solution)/shard_map/ppermute | solution.py:376
  33.6 5.7 %collective-permute-start.9 = (bf16[8,3072]{1,0:T(8,128)(2,1)S(1)}, bf16[8,3072]{1,0:T(8,128)(2,1)S(1)}, u32[]{:S(2)}, u32[]{:S(2)}) collective-permute-start(bf16[8,3072]{1,0:T(8,128)(2,1)S(1)} %get-tuple-element.44), channel_id=1, source_target_pairs={{0,8},{4,12},{8,0},{12,4},{16,24},{20,28},{24,16},{28,20},{32,40},... | collective-permute-start | bytes 147464 | tf_op jit(solution)/shard_map/ppermute | solution.py:368
  34.7 5.3 %collective-permute-start.8 = (bf16[8,3072]{1,0:T(8,128)(2,1)S(1)}, bf16[8,3072]{1,0:T(8,128)(2,1)S(1)}, u32[]{:S(2)}, u32[]{:S(2)}) collective-permute-start(bf16[8,3072]{1,0:T(8,128)(2,1)S(1)} %get-tuple-element.44), channel_id=1, source_target_pairs={{0,12},{4,8},{8,4},{12,0},{16,28},{20,24},{24,20},{28,16},{32,44},... | collective-permute-start | bytes 147464 | tf_op jit(solution)/shard_map/ppermute | solution.py:368
  36.2 4.1 %collective-permute-start.7 = (bf16[8,3072]{1,0:T(8,128)(2,1)S(1)}, bf16[8,3072]{1,0:T(8,128)(2,1)S(1)}, u32[]{:S(2)}, u32[]{:S(2)}) collective-permute-start(bf16[8,3072]{1,0:T(8,128)(2,1)S(1)} %get-tuple-element.44), channel_id=1, source_target_pairs={{0,4},{4,0},{8,12},{12,8},{16,20},{20,16},{24,28},{28,24},{32,36},... | collective-permute-start | bytes 147464 | tf_op jit(solution)/shard_map/ppermute | solution.py:368
  39.3 13.6 %collective-permute-start.15 = (bf16[384,1024]{1,0:T(8,128)(2,1)S(1)}, bf16[384,1024]{1,0:T(8,128)(2,1)S(1)}, u32[]{:S(2)}, u32[]{:S(2)}) collective-permute-start(bf16[384,1024]{1,0:T(8,128)(2,1)S(1)} %product_part.5), channel_id=1, source_target_pairs={{1,0},{2,1},{3,2},{0,3},{5,4},{6,5},{7,6},{4,7},{9,8},{10,9},{11,1... | collective-permute-start | bytes 2359304 | tf_op jit(solution)/shard_map/ppermute | solution.py:376
  44.2 6.1 %collective-permute-start.14 = (bf16[8,3072]{1,0:T(8,128)(2,1)S(1)}, bf16[8,3072]{1,0:T(8,128)(2,1)S(1)}, u32[]{:S(2)}, u32[]{:S(2)}) collective-permute-start(bf16[8,3072]{1,0:T(8,128)(2,1)S(1)} %add_convert_fusion.1), channel_id=1, source_target_pairs={{0,64},{4,68},{8,72},{12,76},{16,80},{20,84},{24,88},{28,92},{32,9... | collective-permute-start | bytes 147464 | tf_op jit(solution)/shard_map/ppermute | solution.py:368
  47.2 5.6 %collective-permute-start.13 = (bf16[8,3072]{1,0:T(8,128)(2,1)S(1)}, bf16[8,3072]{1,0:T(8,128)(2,1)S(1)}, u32[]{:S(2)}, u32[]{:S(2)}) collective-permute-start(bf16[8,3072]{1,0:T(8,128)(2,1)S(1)} %add_convert_fusion.1), channel_id=1, source_target_pairs={{0,96},{4,100},{8,104},{12,108},{16,112},{20,116},{24,120},{28,124... | collective-permute-start | bytes 147464 | tf_op jit(solution)/shard_map/ppermute | solution.py:368
  48.3 4.6 %collective-permute-start.12 = (bf16[8,3072]{1,0:T(8,128)(2,1)S(1)}, bf16[8,3072]{1,0:T(8,128)(2,1)S(1)}, u32[]{:S(2)}, u32[]{:S(2)}) collective-permute-start(bf16[8,3072]{1,0:T(8,128)(2,1)S(1)} %add_convert_fusion.1), channel_id=1, source_target_pairs={{0,32},{4,36},{8,40},{12,44},{16,48},{20,52},{24,56},{28,60},{32,0... | collective-permute-start | bytes 147464 | tf_op jit(solution)/shard_map/ppermute | solution.py:368
  52.9 5.9 %collective-permute-start.16 = (bf16[8,3072]{1,0:T(8,128)(2,1)S(1)}, bf16[8,3072]{1,0:T(8,128)(2,1)S(1)}, u32[]{:S(2)}, u32[]{:S(2)}) collective-permute-start(bf16[8,3072]{1,0:T(8,128)(2,1)S(1)} %add_convert_fusion), channel_id=1, source_target_pairs={{0,16},{4,20},{8,24},{12,28},{16,0},{20,4},{24,8},{28,12},{32,48},... | collective-permute-start | bytes 147464 | tf_op jit(solution)/shard_map/ppermute | solution.py:368
